TPU v7x, 32 devices: a whole 2x2x4 slice. The times are simulated.
32 devices in a mesh: shard: 16 (over z, y, x), rep: 2 (over core).
Axes of the slice: x: 2, y: 2, z: 4, core: 2. Of those that a mesh axis runs over, the one named last changes fastest.
Arguments:
- left: bfloat16 [16384, 1024], P(('shard', 'rep')), may hold values from -110 to 110
- catalog: bfloat16 [32768, 1792], P('shard'), may hold values from -16 to 16
- probes: int32 [32, 25], P(('shard', 'rep')), may hold values from -1 to 127, as said below
- perm: int32 [16384], P(('shard', 'rep')), may hold values from 0 to 16383, as said below
Outputs:
- result: bfloat16 [16384, 768], P(('shard', 'rep'))
Inputs may be any that keep to these rules, and one draw needn't show every extreme that they name: `probes`: each row lists, for each of the 5 owners nearest to its left block's shard index (offsets -2 to 2, modulo the number of shard indices), between 3 and 5 distinct blocks of that owner; all other entries are -1; entries in random order. In every draw some row lists 5 blocks on each of these owners. `perm`: A permutation; the rows of each left block go to each left block exactly 512 // 32 times.
All inputs are finite; a program needn't handle non-finite values.
Results may differ from a plain program's by a relative error of at most 0.0033.
Values may be sent and summed in bfloat16 or wider, within the bound.
A program may use at most 128 MiB of HBM per device.

v0:
```python
import math

import jax
import jax.numpy as jnp
from jax import lax
from jax.sharding import PartitionSpec as P

D = 1024
A = 768
BLK = 256
CB_DEV = 8
REACH = 2
CAP = 5


def shifted(block, axis, distance):
    devices = range(lax.axis_size(axis))
    route = [((i - distance) % len(devices), i) for i in devices]
    return lax.ppermute(block, axis, route)


def slots_for(listed, owner):
    hit = (listed >= 0) & (listed // CB_DEV == owner)
    places = jnp.cumsum(hit.astype(jnp.int32)) - 1
    target = jnp.where(hit, places, CAP)
    filled = jnp.full((CAP + 1,), -1, jnp.int32).at[target].set(jnp.where(hit, listed % CB_DEV, -1))
    slots = filled[:CAP]
    return slots


def group_partial(queries_in, blocks, valid):
    key_part = blocks[:, :, :D]
    value_part = blocks[:, :, D:]
    scores = jnp.einsum("qd,cbd->qcb", queries_in, key_part, preferred_element_type=jnp.float32) * (
        2.5 / math.sqrt(D)
    )
    scores = jnp.where(valid[None, :, None], scores, -jnp.inf)
    group_max = jnp.max(scores, axis=(1, 2))
    expos = jnp.exp(scores - group_max[:, None, None])
    group_total = jnp.sum(expos, axis=(1, 2))
    weights = expos.astype(jnp.bfloat16)
    group_acc = jnp.einsum("qcb,cba->qa", weights, value_part, preferred_element_type=jnp.float32)
    return (group_max, group_total, group_acc)


def combine_groups(parts):
    peak = parts[0][0]
    for part in parts[1:]:
        peak = jnp.maximum(peak, part[0])
    numer = jnp.zeros_like(parts[0][2])
    denom = jnp.zeros_like(parts[0][1])
    for part in parts:
        factor = jnp.exp(part[0] - peak)
        numer = numer + factor[:, None] * part[2]
        denom = denom + factor * part[1]
    return (numer / denom[:, None]).astype(jnp.bfloat16)


def body(left, catalog, probes, perm):
    shard_count = lax.axis_size("shard")
    rep_count = lax.axis_size("rep")
    own_shard = lax.axis_index("shard")
    table = catalog.reshape(CB_DEV, BLK, D + A)
    listed = probes[0]
    parts = []
    for offset in range(-REACH, REACH + 1):
        owner = (own_shard + offset) % shard_count
        slots = slots_for(listed, owner)
        valid = slots >= 0
        if offset == 0:
            parts.append(group_partial(left, table[jnp.maximum(slots, 0)], valid))
        else:
            remote = shifted(table, "shard", -offset)
            parts.append(group_partial(left, remote[jnp.maximum(slots, 0)], valid))
    joined = combine_groups(parts)
    block_rows = left.shape[0]
    rows_each = block_rows // (shard_count * rep_count)
    target_device = perm // block_rows
    target_row = perm % block_rows
    ordering = jnp.argsort(target_device, stable=True)
    outgoing = joined[ordering].reshape(shard_count, rep_count, rows_each, A)
    positions = target_row[ordering].reshape(shard_count, rep_count, rows_each)
    arrived, landing = (
        lax.all_to_all(
            lax.all_to_all(outgoing, "shard", split_axis=0, concat_axis=0, tiled=True),
            "rep",
            split_axis=1,
            concat_axis=1,
            tiled=True,
        ),
        lax.all_to_all(
            lax.all_to_all(positions, "shard", split_axis=0, concat_axis=0, tiled=True),
            "rep",
            split_axis=1,
            concat_axis=1,
            tiled=True,
        ),
    )
    result = (
        jnp.zeros((block_rows, A), jnp.bfloat16).at[landing.reshape(-1)].set(arrived.reshape(-1, A))
    )
    return result


def solution(mesh):
    placed = (
        P(("shard", "rep"), None),
        P("shard", None),
        P(("shard", "rep"), None),
        P(("shard", "rep")),
    )
    return jax.shard_map(
        body, mesh=mesh, in_specs=placed, out_specs=P(("shard", "rep"), None), check_vma=False
    )
```

profile of v0, /device:TPU:5, one launch (start us, length us, event | category | flops | bytes accessed | tf_op | source)
XLA Modules:
  0.0 572.5 jit_solution(14278072935395668203)
XLA Ops:
  0.0 1.2 collective-permute-start.2
  1.5 1.8 collective-permute-start
  3.3 2.1 collective-permute-start.3
  6.1 3.8 sort.17
  9.9 3.5 gather_fusion
  13.4 0.7 reshape.514
  14.1 7.8 %all-to-all-start = ((s32[16,2,16]{2,1,0:T(2,128)}), s32[16,2,16]{2,1,0:T(2,128)S(1)}, u32[]{:S(2)}, u32[]{:S(2)}) async-start(s32[16,2,16]{2,1,0:T(2,128)} %reshape.514), calls=%async_computation | async-start | bytes 32768 | tf_op jit(solution)/shard_map/all_to_all | solution.py:92
  21.9 0.7 copy.52
  24.1 6.3 %gather_fusion.3 = bf16[5,256,1792]{2,1,0:T(8,128)(2,1)} fusion(bf16[8,256,1792]{2,1,0:T(8,128)(2,1)} %bitcast.117, s32[1024]{0:T(1024)S(1)} %pad_clamp_fusion.2), kind=kCustom, calls=%fused_computation.3 | custom fusion | bytes 9175060 | tf_op jit(solution)/shard_map/gather | solution.py:71
  33.1 3.3 fusion.12
  37.1 2.9 fusion.29
  40.0 437.9 %all-to-all-done = s32[16,2,16]{2,1,0:T(2,128)S(1)} async-done(((s32[16,2,16]{2,1,0:T(2,128)}), s32[16,2,16]{2,1,0:T(2,128)S(1)}, u32[]{:S(2)}, u32[]{:S(2)}) %all-to-all-start) | async-done | bytes 2080 | tf_op jit(solution)/shard_map/all_to_all | solution.py:92
  478.6 4.7 all-to-all-start.1
  483.4 6.3 %gather_fusion.4 = bf16[5,256,1792]{2,1,0:T(8,128)(2,1)} fusion(bf16[8,256,1792]{2,1,0:T(8,128)(2,1)} %collective-permute-done.2, s32[1024]{0:T(1024)S(1)} %pad_clamp_fusion.1), kind=kCustom, calls=%fused_computation.4 | custom fusion | bytes 9175060 | tf_op jit(solution)/shard_map/gather | solution.py:74
  489.7 6.3 %gather_fusion.2 = bf16[5,256,1792]{2,1,0:T(8,128)(2,1)} fusion(bf16[8,256,1792]{2,1,0:T(8,128)(2,1)} %collective-permute-done.1, s32[1024]{0:T(1024)S(1)} %pad_clamp_fusion.3), kind=kCustom, calls=%fused_computation.2 | custom fusion | bytes 9175060 | tf_op jit(solution)/shard_map/gather | solution.py:74
  496.0 6.3 %gather_fusion.1 = bf16[5,256,1792]{2,1,0:T(8,128)(2,1)} fusion(bf16[8,256,1792]{2,1,0:T(8,128)(2,1)} %collective-permute-done, s32[1024]{0:T(1024)S(1)} %pad_clamp_fusion.4), kind=kCustom, calls=%fused_computation.1 | custom fusion | bytes 9175060 | tf_op jit(solution)/shard_map/gather | solution.py:74
  502.3 3.5 fusion.13
  506.4 1.6 fusion.11
  508.7 1.6 fusion.10
  510.9 4.2 fusion.27
  515.1 2.5 fusion.31
  517.6 2.6 fusion.33
  520.2 6.4 %gather_fusion.5 = bf16[5,256,1792]{2,1,0:T(8,128)(2,1)} fusion(bf16[8,256,1792]{2,1,0:T(8,128)(2,1)} %collective-permute-done.3, s32[1024]{0:T(1024)S(1)} %pad_clamp_fusion), kind=kCustom, calls=%fused_computation.5 | custom fusion | bytes 9175060 | tf_op jit(solution)/shard_map/gather | solution.py:74
  526.6 3.7 fusion.14
  530.9 0.7 copy-done.2
  531.6 3.5 fusion.37
  535.2 2.7 gather_fusion.6
  537.9 6.4 %all-to-all-start.2 = ((bf16[16,2,16,768]{3,2,1,0:T(8,128)(2,1)}), bf16[16,2,16,768]{3,2,1,0:T(8,128)(2,1)S(1)}, u32[]{:S(2)}, u32[]{:S(2)}) async-start(bf16[16,2,16,768]{3,2,1,0:T(8,128)(2,1)} %bitcast.15), calls=%async_computation.2 | async-start | bytes 1572864 | tf_op jit(solution)/shard_map/all_to_all | solution.py:85
  544.8 0.7 reduce.20
  545.7 16.5 %all-to-all-done.2 = bf16[16,2,16,768]{3,2,1,0:T(8,128)(2,1)S(1)} async-done(((bf16[16,2,16,768]{3,2,1,0:T(8,128)(2,1)}), bf16[16,2,16,768]{3,2,1,0:T(8,128)(2,1)S(1)}, u32[]{:S(2)}, u32[]{:S(2)}) %all-to-all-start.2) | async-done | bytes 786464 | tf_op jit(solution)/shard_map/all_to_all | solution.py:85
  562.3 6.5 %all_to_all.20 = bf16[16,2,16,768]{3,2,0,1:T(8,128)(2,1)S(1)} all-to-all(bf16[16,2,16,768]{3,2,0,1:T(8,128)(2,1)S(1)} %copy.62), channel_id=1, replica_groups=mesh['shard'=16,'rep'=2] {'rep'}, dimensions={1} | all-to-all | bytes 1572864 | tf_op jit(solution)/shard_map/all_to_all | solution.py:84
  568.9 3.6 scatter_custom_fusion.5
  (76 shorter events, 9.7 us)
Async XLA Ops:
  0.0 33.1 %copy-start = (bf16[512,1024]{1,0:T(8,128)(2,1)S(1)}, bf16[512,1024]{1,0:T(8,128)(2,1)}, u32[]{:S(2)}) copy-start(bf16[512,1024]{1,0:T(8,128)(2,1)} %param.4) | copy-start | bytes 3145732
  0.0 23.1 %copy-start.1 = (s32[1,25]{1,0:T(1,128)S(1)}, s32[1,25]{1,0:T(1,128)}, u32[]{:S(2)}) copy-start(s32[1,25]{1,0:T(1,128)} %param.6) | copy-start | bytes 304
  0.0 483.4 %collective-permute-start.2 = (bf16[8,256,1792]{2,1,0:T(8,128)(2,1)}, bf16[8,256,1792]{2,1,0:T(8,128)(2,1)}, u32[]{:S(2)}, u32[]{:S(2)}) collective-permute-start(bf16[8,256,1792]{2,1,0:T(8,128)(2,1)} %bitcast.113), channel_id=1, source_target_pairs={{2,0},{4,2},{6,4},{8,6},{10,8},{12,10},{14,12},{16,14},{18,16},{20... | collective-permute-start | bytes 22020104 | tf_op jit(solution)/shard_map/ppermute | solution.py:19
  1.2 488.5 %collective-permute-start.1 = (bf16[8,256,1792]{2,1,0:T(8,128)(2,1)}, bf16[8,256,1792]{2,1,0:T(8,128)(2,1)}, u32[]{:S(2)}, u32[]{:S(2)}) collective-permute-start(bf16[8,256,1792]{2,1,0:T(8,128)(2,1)} %bitcast.114), channel_id=1, source_target_pairs={{30,0},{0,2},{2,4},{4,6},{6,8},{8,10},{10,12},{12,14},{14,16},{16,... | collective-permute-start | bytes 22020104 | tf_op jit(solution)/shard_map/ppermute | solution.py:19
  1.5 494.5 %collective-permute-start = (bf16[8,256,1792]{2,1,0:T(8,128)(2,1)}, bf16[8,256,1792]{2,1,0:T(8,128)(2,1)}, u32[]{:S(2)}, u32[]{:S(2)}) collective-permute-start(bf16[8,256,1792]{2,1,0:T(8,128)(2,1)} %bitcast.115), channel_id=1, source_target_pairs={{28,0},{30,2},{0,4},{2,6},{4,8},{6,10},{8,12},{10,14},{12,16},{14,... | collective-permute-start | bytes 22020104 | tf_op jit(solution)/shard_map/ppermute | solution.py:19
  3.3 516.9 %collective-permute-start.3 = (bf16[8,256,1792]{2,1,0:T(8,128)(2,1)}, bf16[8,256,1792]{2,1,0:T(8,128)(2,1)}, u32[]{:S(2)}, u32[]{:S(2)}) collective-permute-start(bf16[8,256,1792]{2,1,0:T(8,128)(2,1)} %bitcast.116), channel_id=1, source_target_pairs={{4,0},{6,2},{8,4},{10,6},{12,8},{14,10},{16,12},{18,14},{20,16},{2... | collective-permute-start | bytes 22020104 | tf_op jit(solution)/shard_map/ppermute | solution.py:19
  14.1 463.9 %all-to-all-start = ((s32[16,2,16]{2,1,0:T(2,128)}), s32[16,2,16]{2,1,0:T(2,128)S(1)}, u32[]{:S(2)}, u32[]{:S(2)}) async-start(s32[16,2,16]{2,1,0:T(2,128)} %reshape.514), calls=%async_computation | async-start | bytes 32768 | tf_op jit(solution)/shard_map/all_to_all | solution.py:92
  478.6 59.2 %all-to-all-start.1 = ((s32[2,1,256]{2,1,0:T(1,128)}), s32[2,1,256]{2,1,0:T(1,128)S(1)}, u32[]{:S(2)}, u32[]{:S(2)}) async-start(s32[2,1,256]{2,1,0:T(1,128)} %reshape.653), calls=%async_computation.1 | async-start | bytes 4096 | tf_op jit(solution)/shard_map/all_to_all | solution.py:91
  496.0 10.4 %slice-start = ((s8[4587520]{0:T(1024)(128)(4,1)}), s8[393216]{0:T(1024)(128)(4,1)S(1)}, s32[]{:S(2)}) async-start(s8[4587520]{0:T(1024)(128)(4,1)} %bitcast.109), calls=%async_computation.4 | async-start | bytes 786432
  502.3 4.1 slice-start.1
  505.8 2.9 slice-start.2
  506.4 2.2 slice-start.3
  526.5 4.3 copy-start.3
  526.6 4.3 copy-start.4
  530.2 1.4 copy-start.2
  537.9 24.4 %all-to-all-start.2 = ((bf16[16,2,16,768]{3,2,1,0:T(8,128)(2,1)}), bf16[16,2,16,768]{3,2,1,0:T(8,128)(2,1)S(1)}, u32[]{:S(2)}, u32[]{:S(2)}) async-start(bf16[16,2,16,768]{3,2,1,0:T(8,128)(2,1)} %bitcast.15), calls=%async_computation.2 | async-start | bytes 1572864 | tf_op jit(solution)/shard_map/all_to_all | solution.py:85
where the time goes:
time: 574 us; the launch traced here: 572 us
  waiting for transfers between devices  454 us (79%)
  local copies, waits for them, and re-layouts  48.3 us (8%)
  matrix products  29.4 us (5%)
  starting transfers between devices  24.4 us (4%)
  other arithmetic  9.02 us (2%)
  blocking collectives  6.54 us (1%)
    all_to_all x1, waiting for transfers between devices, body(): lax.all_to_all(positions, 'shard', split_axis=0, concat_axis=0, tiled=True)  438 us
    gather x4, local copies, waits for them, and re-layouts, body(): parts.append(group_partial(left, remote[jnp.maximum(slots, 0)], valid))  25.3 us
    all_to_all x1, waiting for transfers between devices, body(): lax.all_to_all(outgoing, 'shard', split_axis=0, concat_axis=0, tiled=True)  16.5 us
    dot_general x5, matrix products, group_partial(): jnp.einsum('qcb,cba->qa', weights, value_part, preferred_element_type=jnp...  15.7 us
    dot_general x5, matrix products, group_partial(): jnp.einsum('qd,cbd->qcb', queries_in, key_part, preferred_element_type=jn...  13.7 us
  transfers between devices with their start and end apart: 7, of which 2 were waited for; matrix products, arithmetic and copies ran while one was open for 14% of the time, Pallas kernels for 0%

commit v1 on v0

v1 whole, which is shorter than its diff:
```python
import math

import jax
import jax.numpy as jnp
from jax import lax
from jax.experimental import pallas as pl
from jax.experimental.pallas import tpu as pltpu
from jax.sharding import PartitionSpec as P

D = 1024
A = 768
BLK = 256
CB_DEV = 8
REACH = 2
CAP = 5
SCALE = 2.5 / math.sqrt(D)
NT = (((1,), (1,)), ((), ()))


def shifted(block, axis, distance):
    devices = range(lax.axis_size(axis))
    route = [((i - distance) % len(devices), i) for i in devices]
    return lax.ppermute(block, axis, route)


def slots_for(listed, owner):
    hit = (listed >= 0) & (listed // CB_DEV == owner)
    places = jnp.cumsum(hit.astype(jnp.int32)) - 1
    chosen = hit[None, :] & (places[None, :] == jnp.arange(CAP)[:, None])
    return jnp.max(jnp.where(chosen, listed[None, :] % CB_DEV, -1), axis=1)


def group_kernel(slots_ref, q_ref, *refs):
    blocks, (acc_ref, stat_ref) = refs[:CAP], refs[CAP:]
    q = q_ref[...]
    scores = []
    for j in range(CAP):
        s = lax.dot_general(q, blocks[j][:, :D], NT, preferred_element_type=jnp.float32) * SCALE
        scores.append(jnp.where(slots_ref[j] >= 0, s, -jnp.inf))
    peak = scores[0]
    for s in scores[1:]:
        peak = jnp.maximum(peak, s)
    peak = jnp.max(peak, axis=1, keepdims=True)
    total = jnp.zeros_like(peak)
    acc = None
    for j in range(CAP):
        e = jnp.exp(scores[j] - peak)
        total = total + jnp.sum(e, axis=1, keepdims=True)
        part = jnp.dot(e.astype(jnp.bfloat16), blocks[j][:, D:], preferred_element_type=jnp.float32)
        acc = part if acc is None else acc + part
    acc_ref[...] = acc.astype(acc_ref.dtype)
    lane = lax.broadcasted_iota(jnp.int32, (q.shape[0], 128), 1)
    stat = jnp.where(lane == 0, peak, total)
    stat_ref[...] = stat.T[:8, :]


def group_partial(q, catalog, slots, dtype):
    rows = q.shape[0]
    chunk = 256
    return pl.pallas_call(
        group_kernel,
        grid_spec=pltpu.PrefetchScalarGridSpec(
            num_scalar_prefetch=1,
            grid=(rows // chunk,),
            in_specs=[pl.BlockSpec((chunk, D), lambda i, s: (i, 0))]
            + [
                pl.BlockSpec((BLK, D + A), lambda i, s, j=j: (jnp.maximum(s[j], 0), 0))
                for j in range(CAP)
            ],
            out_specs=[
                pl.BlockSpec((chunk, A), lambda i, s: (i, 0)),
                pl.BlockSpec((8, chunk), lambda i, s: (0, i)),
            ],
        ),
        out_shape=[
            jax.ShapeDtypeStruct((rows, A), dtype),
            jax.ShapeDtypeStruct((8, rows), jnp.float32),
        ],
        compiler_params=pltpu.CompilerParams(vmem_limit_bytes=40 * 1024 * 1024),
        cost_estimate=pl.CostEstimate(
            flops=2 * rows * CAP * BLK * (D + A),
            bytes_accessed=CAP * BLK * (D + A) * 2 + rows * (D + 2 * A) * 2,
            transcendentals=rows * CAP * BLK,
        ),
    )(slots, q, *([catalog] * CAP))


def body(left, catalog, probes, perm):
    shard_count = lax.axis_size("shard")
    rep_count = lax.axis_size("rep")
    own = lax.axis_index("shard")
    block_rows = left.shape[0]
    devices = shard_count * rep_count
    rows_each = block_rows // devices
    offsets = (2, -2, 1, -1)
    moved = {k: shifted(left, "shard", k) for k in offsets}
    lists = {k: shifted(probes, "shard", k) for k in offsets}

    target_device = perm // block_rows
    target_row = perm % block_rows
    index = jnp.arange(block_rows)
    earlier = (target_device[:, None] == target_device[None, :]) & (index[None, :] < index[:, None])
    place = target_device * rows_each + jnp.sum(earlier.astype(jnp.int32), axis=1)
    order = place[None, :] == index[:, None]
    positions = jnp.sum(jnp.where(order, target_row[None, :], 0), axis=1).astype(jnp.int32)
    landing = lax.all_to_all(
        positions.reshape(devices, rows_each), ("shard", "rep"), 0, 0, tiled=True
    ).reshape(-1)

    parts = [group_partial(left, catalog, slots_for(probes[0], own), jnp.float32)]
    for k in offsets:
        acc, stat = group_partial(
            moved[k], catalog, slots_for(lists[k][0], own), jnp.bfloat16
        )
        parts.append((shifted(acc, "shard", -k), shifted(stat[:2], "shard", -k)))
    peak = parts[0][1][0]
    for part in parts[1:]:
        peak = jnp.maximum(peak, part[1][0])
    numer = jnp.zeros((block_rows, A), jnp.float32)
    denom = jnp.zeros((block_rows,), jnp.float32)
    for acc, stat in parts:
        factor = jnp.exp(stat[0] - peak)
        numer = numer + factor[:, None] * acc.astype(jnp.float32)
        denom = denom + factor * stat[1]
    joined = (numer / denom[:, None]).astype(jnp.bfloat16)

    outgoing = jnp.dot(
        order.astype(jnp.bfloat16), joined, preferred_element_type=jnp.float32
    ).astype(jnp.bfloat16)
    arrived = lax.all_to_all(
        outgoing.reshape(devices, rows_each, A), ("shard", "rep"), 0, 0, tiled=True
    ).reshape(block_rows, A)
    spread = (landing[None, :] == index[:, None]).astype(jnp.bfloat16)
    return jnp.dot(spread, arrived, preferred_element_type=jnp.float32).astype(jnp.bfloat16)


def solution(mesh):
    placed = (
        P(("shard", "rep"), None),
        P("shard", None),
        P(("shard", "rep"), None),
        P(("shard", "rep")),
    )
    return jax.shard_map(
        body, mesh=mesh, in_specs=placed, out_specs=P(("shard", "rep"), None), check_vma=False
    )
```

time: 574 us -> 191 us (0.33)
  waiting for transfers between devices: 454 us -> 91.2 us
  local copies, waits for them, and re-layouts: 48.3 us -> 9.22 us
  Pallas kernels: 0 us -> 30.3 us
  matrix products: 29.4 us -> 3.8 us
  starting transfers between devices: 24.4 us -> 49.9 us
  blocking collectives: 6.54 us -> 0 us
    all_to_all x3 -> x2, waiting for transfers between devices: 454 us -> 18.6 us  [the longest x1 18.6 us: body(): lax.all_to_all(outgoing.reshape(devices, rows_each, A), ('shard', 'rep'),...]
    ppermute x4 -> x16, waiting for transfers between devices: 0.01 us -> 72.6 us  [shifted(): return lax.ppermute(block, axis, route)]
    gather x7 -> x0, local copies, waits for them, and re-layouts: 37.7 us -> none  [the longest x4 25.3 us: body(): parts.append(group_partial(left, remote[jnp.maximum(slots, 0)], valid))]
    pallas_call x0 -> x5, Pallas kernels: none -> 30.3 us  [group_partial(): pl.pallas_call(group_kernel, grid_spec=pltpu.PrefetchScalarGridSpec(num_s...]
    dot_general x10 -> x2, matrix products: 29.4 us -> 3.8 us  [the longest x1 2.33 us: body(): jnp.dot(order.astype(jnp.bfloat16), joined, preferred_element_type=jnp.fl...]
    ppermute x4 -> x16, starting transfers between devices: 5.44 us -> 30.8 us  [shifted(): return lax.ppermute(block, axis, route)]
    scatter x6 -> x0, local copies, waits for them, and re-layouts: 6.8 us -> none  [the longest x1 3.56 us: body(): jnp.zeros((block_rows, A), jnp.bfloat16).at[landing.reshape(-1)]]
    all_to_all x1 -> x0, blocking collectives: 6.54 us -> none  [body(): lax.all_to_all(lax.all_to_all(outgoing, 'shard', split_axis=0, concat_axi...]
  transfers between devices with their start and end apart: 7 -> 18, of which waited for: 2 -> 4; matrix products, arithmetic and copies ran while one was open for 14% -> 4% of each run, Pallas kernels for 0% -> 16%
where the time goes in v1:
time: 191 us; the launch traced here: 190 us
  waiting for transfers between devices  91.2 us (48%)
  starting transfers between devices  49.9 us (26%)
  Pallas kernels  30.3 us (16%)
  local copies, waits for them, and re-layouts  9.22 us (5%)
  other arithmetic  4.71 us (2%)
  matrix products  3.8 us (2%)
    ppermute x16, waiting for transfers between devices, shifted(): return lax.ppermute(block, axis, route)  72.6 us
    ppermute x16, starting transfers between devices, shifted(): return lax.ppermute(block, axis, route)  30.8 us
    pallas_call x5, Pallas kernels, group_partial(): pl.pallas_call(group_kernel, grid_spec=pltpu.PrefetchScalarGridSpec(num_s...  30.3 us
    all_to_all x1, waiting for transfers between devices, body(): lax.all_to_all(outgoing.reshape(devices, rows_each, A), ('shard', 'rep'),...  18.6 us
    all_to_all x1, starting transfers between devices, body(): lax.all_to_all(positions.reshape(devices, rows_each), ('shard', 'rep'), 0...  11.3 us
    all_to_all x1, starting transfers between devices, body(): lax.all_to_all(outgoing.reshape(devices, rows_each, A), ('shard', 'rep'),...  7.78 us
    unnamed x12, local copies, waits for them, and re-layouts  7.32 us
  transfers between devices with their start and end apart: 18, of which 4 were waited for; matrix products, arithmetic and copies ran while one was open for 4% of the time, Pallas kernels for 16%

profile of v1, /device:TPU:5, one launch (start us, length us, event | category | flops | bytes accessed | tf_op | source)
XLA Modules:
  0.0 189.5 jit_solution(13851726047281122220)
XLA Ops:
  0.0 2.4 %collective-permute-start = (s32[1,25]{1,0:T(1,128)}, s32[1,25]{1,0:T(1,128)S(1)}, u32[]{:S(2)}, u32[]{:S(2)}) collective-permute-start(s32[1,25]{1,0:T(1,128)} %param.6), channel_id=1, source_target_pairs={{28,0},{30,2},{0,4},{2,6},{4,8},{6,10},{8,12},{10,14},{12,16},{14,... | collective-permute-start | bytes 308 | tf_op jit(solution)/shard_map/ppermute | solution.py:23
  2.4 3.1 %collective-permute-start.9 = (s32[1,25]{1,0:T(1,128)}, s32[1,25]{1,0:T(1,128)S(1)}, u32[]{:S(2)}, u32[]{:S(2)}) collective-permute-start(s32[1,25]{1,0:T(1,128)} %param.6), channel_id=1, source_target_pairs={{2,0},{4,2},{6,4},{8,6},{10,8},{12,10},{14,12},{16,14},{18,16},{20... | collective-permute-start | bytes 308 | tf_op jit(solution)/shard_map/ppermute | solution.py:23
  5.4 0.7 add_select_fusion
  6.1 0.3 convert_reduce_fusion
  6.4 0.2 select_reduce_fusion
  6.6 0.7 all_to_all.9
  7.3 11.3 %all-to-all-start = ((s32[32,1,16]{2,1,0:T(1,128)}), s32[32,1,16]{2,1,0:T(1,128)S(1)}, u32[]{:S(2)}, u32[]{:S(2)}) async-start(s32[32,1,16]{2,1,0:T(1,128)} %bitcast), calls=%async_computation | async-start | bytes 32768 | tf_op jit(solution)/shard_map/all_to_all | solution.py:106
  18.7 0.7 fusion.9
  19.4 0.7 convert_bitcast_fusion.4
  20.5 3.1 %copy-done = bf16[2048,1792]{1,0:T(8,128)(2,1)S(1)} copy-done((bf16[2048,1792]{1,0:T(8,128)(2,1)S(1)}, bf16[2048,1792]{1,0:T(8,128)(2,1)}, u32[]{:S(2)}) %copy-start) | copy-done | bytes 7340056
  23.5 6.7 %shard_map.46 = (f32[512,768]{1,0:T(8,128)S(1)}, f32[8,512]{1,0:T(8,128)S(1)}) custom-call(s32[5]{0:T(128)S(1)} %select_reduce_fusion.5.slots_ref, bf16[512,1024]{1,0:T(8,128)(2,1)} %q_ref.1, bf16[2048,1792]{1,0:T(8,128)(2,1)S(1)} %copy-done, bf16[2048,1792]{1,0:T(8,128)(2,1)S(1)} %copy-done, bf16[2048,1792]{1,0:T(8,128)(2,1)S(1)} %copy-done, ...), custom_call_target="tpu_custom_call" | custom-call | flops 2348810240 | bytes 7208960 | tf_op jit(solution)/shard_map/pallas_call | solution.py:60
  30.2 1.1 copy-done.2
  31.4 2.3 %collective-permute-start.1 = (bf16[512,1024]{1,0:T(8,128)(2,1)}, bf16[512,1024]{1,0:T(8,128)(2,1)}, u32[]{:S(2)}, u32[]{:S(2)}) collective-permute-start(bf16[512,1024]{1,0:T(8,128)(2,1)} %q_ref.1), channel_id=1, source_target_pairs={{28,0},{30,2},{0,4},{2,6},{4,8},{6,10},{8,12},{10,14},{12,16},{14,... | collective-permute-start | bytes 3145736 | tf_op jit(solution)/shard_map/ppermute | solution.py:23
  33.8 2.9 %collective-permute-start.10 = (bf16[512,1024]{1,0:T(8,128)(2,1)}, bf16[512,1024]{1,0:T(8,128)(2,1)S(1)}, u32[]{:S(2)}, u32[]{:S(2)}) collective-permute-start(bf16[512,1024]{1,0:T(8,128)(2,1)} %q_ref.1), channel_id=1, source_target_pairs={{2,0},{4,2},{6,4},{8,6},{10,8},{12,10},{14,12},{16,14},{18,16},{20... | collective-permute-start | bytes 3145736 | tf_op jit(solution)/shard_map/ppermute | solution.py:23
  38.4 25.7 %collective-permute-done.4.q_ref = bf16[512,1024]{1,0:T(8,128)(2,1)S(1)} collective-permute-done((bf16[512,1024]{1,0:T(8,128)(2,1)}, bf16[512,1024]{1,0:T(8,128)(2,1)S(1)}, u32[]{:S(2)}, u32[]{:S(2)}) %collective-permute-start.4) | collective-permute-done | bytes 1048608 | tf_op jit(solution)/shard_map/ppermute | solution.py:23
  64.0 3.1 %copy-done.1 = bf16[2048,1792]{1,0:T(8,128)(2,1)S(1)} copy-done((bf16[2048,1792]{1,0:T(8,128)(2,1)S(1)}, bf16[2048,1792]{1,0:T(8,128)(2,1)}, u32[]{:S(2)}) %copy-start.1) | copy-done | bytes 7340056
  67.1 5.6 %shard_map.48 = (bf16[512,768]{1,0:T(8,128)(2,1)S(1)}, f32[8,512]{1,0:T(8,128)S(1)}) custom-call(s32[5]{0:T(128)S(1)} %select_reduce_fusion.3.slots_ref, bf16[512,1024]{1,0:T(8,128)(2,1)S(1)} %collective-permute-done.4.q_ref, bf16[2048,1792]{1,0:T(8,128)(2,1)S(1)} %copy-done.1, bf16[2048,1792]{1,0:T(8,128)(2,1)S(1)} %copy-done.1, ...), custom_call_target="tpu_custom_call" | custom-call | flops 2348810240 | bytes 7208960 | tf_op jit(solution)/shard_map/pallas_call | solution.py:60
  72.7 3.1 %collective-permute-start.5 = (f32[2,512]{1,0:T(2,128)S(1)}, f32[2,512]{1,0:T(2,128)S(1)}, u32[]{:S(2)}, u32[]{:S(2)}) collective-permute-start(f32[2,512]{1,0:T(2,128)S(1)} %slice.50), channel_id=1, source_target_pairs={{28,0},{30,2},{0,4},{2,6},{4,8},{6,10},{8,12},{10,14},{12,16},{14,... | collective-permute-start | bytes 12296 | tf_op jit(solution)/shard_map/ppermute | solution.py:23
  76.0 14.1 %collective-permute-done.1.q_ref = bf16[512,1024]{1,0:T(8,128)(2,1)} collective-permute-done((bf16[512,1024]{1,0:T(8,128)(2,1)}, bf16[512,1024]{1,0:T(8,128)(2,1)}, u32[]{:S(2)}, u32[]{:S(2)}) %collective-permute-start.1) | collective-permute-done | bytes 1048608 | tf_op jit(solution)/shard_map/ppermute | solution.py:23
  90.1 6.7 %shard_map.47 = (bf16[512,768]{1,0:T(8,128)(2,1)S(1)}, f32[8,512]{1,0:T(8,128)S(1)}) custom-call(s32[5]{0:T(128)S(1)} %select_reduce_fusion.4.slots_ref, bf16[512,1024]{1,0:T(8,128)(2,1)} %collective-permute-done.1.q_ref, bf16[2048,1792]{1,0:T(8,128)(2,1)S(1)} %copy-done.1, bf16[2048,1792]{1,0:T(8,128)(2,1)S(1)} %copy-done.1, ...), custom_call_target="tpu_custom_call" | custom-call | flops 2348810240 | bytes 7208960 | tf_op jit(solution)/shard_map/pallas_call | solution.py:60
  96.8 5.9 %collective-permute-start.12 = (bf16[512,768]{1,0:T(8,128)(2,1)S(1)}, bf16[512,768]{1,0:T(8,128)(2,1)S(1)}, u32[]{:S(2)}, u32[]{:S(2)}) collective-permute-start(bf16[512,768]{1,0:T(8,128)(2,1)S(1)} %get-tuple-element.21), channel_id=1, source_target_pairs={{4,0},{6,2},{8,4},{10,6},{12,8},{14,10},{16,12},{18,14},{20,16},{2... | collective-permute-start | bytes 2359304 | tf_op jit(solution)/shard_map/ppermute | solution.py:23
  102.7 5.7 %shard_map.50 = (bf16[512,768]{1,0:T(8,128)(2,1)S(1)}, f32[8,512]{1,0:T(8,128)S(1)}) custom-call(s32[5]{0:T(128)S(1)} %select_reduce_fusion.1.slots_ref, bf16[512,1024]{1,0:T(8,128)(2,1)S(1)} %collective-permute-done.10.q_ref, bf16[2048,1792]{1,0:T(8,128)(2,1)S(1)} %bitcast.40, bf16[2048,1792]{1,0:T(8,128)(2,1)S(1)} %bitcast.40, ...), custom_call_target="tpu_custom_call" | custom-call | flops 2348810240 | bytes 7208960 | tf_op jit(solution)/shard_map/pallas_call | solution.py:60
  108.4 7.3 %collective-permute-start.11 = (f32[2,512]{1,0:T(2,128)S(1)}, f32[2,512]{1,0:T(2,128)S(1)}, u32[]{:S(2)}, u32[]{:S(2)}) collective-permute-start(f32[2,512]{1,0:T(2,128)S(1)} %slice.54), channel_id=1, source_target_pairs={{30,0},{0,2},{2,4},{4,6},{6,8},{8,10},{10,12},{12,14},{14,16},{16,... | collective-permute-start | bytes 12296 | tf_op jit(solution)/shard_map/ppermute | solution.py:23
  115.7 5.7 %shard_map.49 = (bf16[512,768]{1,0:T(8,128)(2,1)S(1)}, f32[8,512]{1,0:T(8,128)S(1)}) custom-call(s32[5]{0:T(128)S(1)} %select_reduce_fusion.2.slots_ref, bf16[512,1024]{1,0:T(8,128)(2,1)S(1)} %collective-permute-done.7.q_ref, bf16[2048,1792]{1,0:T(8,128)(2,1)S(1)} %bitcast.40, bf16[2048,1792]{1,0:T(8,128)(2,1)S(1)} %bitcast.40, ...), custom_call_target="tpu_custom_call" | custom-call | flops 2348810240 | bytes 7208960 | tf_op jit(solution)/shard_map/pallas_call | solution.py:60
  121.4 3.4 %collective-permute-start.15 = (bf16[512,768]{1,0:T(8,128)(2,1)S(1)}, bf16[512,768]{1,0:T(8,128)(2,1)S(1)}, u32[]{:S(2)}, u32[]{:S(2)}) collective-permute-start(bf16[512,768]{1,0:T(8,128)(2,1)S(1)} %get-tuple-element.24), channel_id=1, source_target_pairs={{30,0},{0,2},{2,4},{4,6},{6,8},{8,10},{10,12},{12,14},{14,16},{16,... | collective-permute-start | bytes 2359304 | tf_op jit(solution)/shard_map/ppermute | solution.py:23
  125.0 32.9 %collective-permute-done.8 = f32[2,512]{1,0:T(2,128)S(1)} collective-permute-done((f32[2,512]{1,0:T(2,128)S(1)}, f32[2,512]{1,0:T(2,128)S(1)}, u32[]{:S(2)}, u32[]{:S(2)}) %collective-permute-start.8) | collective-permute-done | bytes 4128 | tf_op jit(solution)/shard_map/ppermute | solution.py:23
  157.9 2.3 %convolution_convert_fusion.1 = bf16[512,768]{1,0:T(8,128)(2,1)} fusion(bf16[512,768]{1,0:T(8,128)(2,1)S(1)} %collective-permute-done.15, bf16[512,768]{1,0:T(8,128)(2,1)S(1)} %collective-permute-done.14, bf16[512,768]{1,0:T(8,128)(2,1)S(1)} %collective-permute-done.13, bf16[512,768]{1,0:T(8,128)(2,1)S(1)} %collective-permute-done.12, ...), kind=kOutput, calls=%fused_computation.2 | convolution fusion | flops 409206784 | bytes 5519360 | tf_op jit(solution)/shard_map/dot_general | solution.py:127
  160.2 7.8 %all-to-all-start.1 = ((bf16[32,16,768]{2,1,0:T(8,128)(2,1)}), bf16[32,16,768]{2,1,0:T(8,128)(2,1)S(1)}, u32[]{:S(2)}, u32[]{:S(2)}) async-start(bf16[32,16,768]{2,1,0:T(8,128)(2,1)} %bitcast.26), calls=%async_computation.1 | async-start | bytes 1572864 | tf_op jit(solution)/shard_map/all_to_all | solution.py:130
  168.0 0.6 broadcast.415
  168.6 0.7 reduce.13
  169.4 18.6 %all-to-all-done.1 = bf16[32,16,768]{2,1,0:T(8,128)(2,1)S(1)} async-done(((bf16[32,16,768]{2,1,0:T(8,128)(2,1)}), bf16[32,16,768]{2,1,0:T(8,128)(2,1)S(1)}, u32[]{:S(2)}, u32[]{:S(2)}) %all-to-all-start.1) | async-done | bytes 786464 | tf_op jit(solution)/shard_map/all_to_all | solution.py:130
  188.1 1.5 convolution_convert_fusion
  (72 shorter events, 2.6 us)
Async XLA Ops:
  0.0 36.9 %collective-permute-start.3 = (s32[1,25]{1,0:T(1,128)}, s32[1,25]{1,0:T(1,128)S(1)}, u32[]{:S(2)}, u32[]{:S(2)}) collective-permute-start(s32[1,25]{1,0:T(1,128)} %param.6), channel_id=1, source_target_pairs={{4,0},{6,2},{8,4},{10,6},{12,8},{14,10},{16,12},{18,14},{20,16},{2... | collective-permute-start | bytes 308 | tf_op jit(solution)/shard_map/ppermute | solution.py:23
  0.0 31.4 %collective-permute-start = (s32[1,25]{1,0:T(1,128)}, s32[1,25]{1,0:T(1,128)S(1)}, u32[]{:S(2)}, u32[]{:S(2)}) collective-permute-start(s32[1,25]{1,0:T(1,128)} %param.6), channel_id=1, source_target_pairs={{28,0},{30,2},{0,4},{2,6},{4,8},{6,10},{8,12},{10,14},{12,16},{14,... | collective-permute-start | bytes 308 | tf_op jit(solution)/shard_map/ppermute | solution.py:23
  2.4 31.4 %collective-permute-start.9 = (s32[1,25]{1,0:T(1,128)}, s32[1,25]{1,0:T(1,128)S(1)}, u32[]{:S(2)}, u32[]{:S(2)}) collective-permute-start(s32[1,25]{1,0:T(1,128)} %param.6), channel_id=1, source_target_pairs={{2,0},{4,2},{6,4},{8,6},{10,8},{12,10},{14,12},{16,14},{18,16},{20... | collective-permute-start | bytes 308 | tf_op jit(solution)/shard_map/ppermute | solution.py:23
  5.4 31.2 %collective-permute-start.6 = (s32[1,25]{1,0:T(1,128)}, s32[1,25]{1,0:T(1,128)S(1)}, u32[]{:S(2)}, u32[]{:S(2)}) collective-permute-start(s32[1,25]{1,0:T(1,128)} %param.6), channel_id=1, source_target_pairs={{30,0},{0,2},{2,4},{4,6},{6,8},{8,10},{10,12},{12,14},{14,16},{16,... | collective-permute-start | bytes 308 | tf_op jit(solution)/shard_map/ppermute | solution.py:23
  7.3 153.0 %all-to-all-start = ((s32[32,1,16]{2,1,0:T(1,128)}), s32[32,1,16]{2,1,0:T(1,128)S(1)}, u32[]{:S(2)}, u32[]{:S(2)}) async-start(s32[32,1,16]{2,1,0:T(1,128)} %bitcast), calls=%async_computation | async-start | bytes 32768 | tf_op jit(solution)/shard_map/all_to_all | solution.py:106
  18.6 45.4 %collective-permute-start.4 = (bf16[512,1024]{1,0:T(8,128)(2,1)}, bf16[512,1024]{1,0:T(8,128)(2,1)S(1)}, u32[]{:S(2)}, u32[]{:S(2)}) collective-permute-start(bf16[512,1024]{1,0:T(8,128)(2,1)} %q_ref.1), channel_id=1, source_target_pairs={{4,0},{6,2},{8,4},{10,6},{12,8},{14,10},{16,12},{18,14},{20,16},{2... | collective-permute-start | bytes 3145736 | tf_op jit(solution)/shard_map/ppermute | solution.py:23
  20.4 3.1 %copy-start = (bf16[2048,1792]{1,0:T(8,128)(2,1)S(1)}, bf16[2048,1792]{1,0:T(8,128)(2,1)}, u32[]{:S(2)}) copy-start(bf16[2048,1792]{1,0:T(8,128)(2,1)} %refs_4_.9) | copy-start | bytes 22020100
  30.2 1.2 copy-start.2
  31.4 58.7 %collective-permute-start.1 = (bf16[512,1024]{1,0:T(8,128)(2,1)}, bf16[512,1024]{1,0:T(8,128)(2,1)}, u32[]{:S(2)}, u32[]{:S(2)}) collective-permute-start(bf16[512,1024]{1,0:T(8,128)(2,1)} %q_ref.1), channel_id=1, source_target_pairs={{28,0},{30,2},{0,4},{2,6},{4,8},{6,10},{8,12},{10,14},{12,16},{14,... | collective-permute-start | bytes 3145736 | tf_op jit(solution)/shard_map/ppermute | solution.py:23
  33.8 63.1 %collective-permute-start.10 = (bf16[512,1024]{1,0:T(8,128)(2,1)}, bf16[512,1024]{1,0:T(8,128)(2,1)S(1)}, u32[]{:S(2)}, u32[]{:S(2)}) collective-permute-start(bf16[512,1024]{1,0:T(8,128)(2,1)} %q_ref.1), channel_id=1, source_target_pairs={{2,0},{4,2},{6,4},{8,6},{10,8},{12,10},{14,12},{16,14},{18,16},{20... | collective-permute-start | bytes 3145736 | tf_op jit(solution)/shard_map/ppermute | solution.py:23
  36.7 71.7 %collective-permute-start.7 = (bf16[512,1024]{1,0:T(8,128)(2,1)}, bf16[512,1024]{1,0:T(8,128)(2,1)S(1)}, u32[]{:S(2)}, u32[]{:S(2)}) collective-permute-start(bf16[512,1024]{1,0:T(8,128)(2,1)} %q_ref.1), channel_id=1, source_target_pairs={{30,0},{0,2},{2,4},{4,6},{6,8},{8,10},{10,12},{12,14},{14,16},{16,... | collective-permute-start | bytes 3145736 | tf_op jit(solution)/shard_map/ppermute | solution.py:23
  64.0 3.1 %copy-start.1 = (bf16[2048,1792]{1,0:T(8,128)(2,1)S(1)}, bf16[2048,1792]{1,0:T(8,128)(2,1)}, u32[]{:S(2)}) copy-start(bf16[2048,1792]{1,0:T(8,128)(2,1)} %refs_4_.9) | copy-start | bytes 22020100
  72.7 48.7 %collective-permute-start.5 = (f32[2,512]{1,0:T(2,128)S(1)}, f32[2,512]{1,0:T(2,128)S(1)}, u32[]{:S(2)}, u32[]{:S(2)}) collective-permute-start(f32[2,512]{1,0:T(2,128)S(1)} %slice.50), channel_id=1, source_target_pairs={{28,0},{30,2},{0,4},{2,6},{4,8},{6,10},{8,12},{10,14},{12,16},{14,... | collective-permute-start | bytes 12296 | tf_op jit(solution)/shard_map/ppermute | solution.py:23
  75.9 26.8 %slice-start = ((s8[7340032]{0:T(1024)(128)(4,1)}), s8[4194304]{0:T(1024)(128)(4,1)S(1)}, s32[]{:S(2)}) async-start(s8[7340032]{0:T(1024)(128)(4,1)} %bitcast.39), calls=%async_computation.2 | async-start | bytes 8388608
  75.9 26.8 %slice-start.1 = ((s8[7340032]{0:T(1024)(128)(4,1)}), s8[3145728]{0:T(1024)(128)(4,1)S(1)}, s32[]{:S(2)}) async-start(s8[7340032]{0:T(1024)(128)(4,1)} %bitcast.39), calls=%async_computation.3 | async-start | bytes 6291456
  75.9 82.0 %collective-permute-start.13 = (bf16[512,768]{1,0:T(8,128)(2,1)S(1)}, bf16[512,768]{1,0:T(8,128)(2,1)S(1)}, u32[]{:S(2)}, u32[]{:S(2)}) collective-permute-start(bf16[512,768]{1,0:T(8,128)(2,1)S(1)} %get-tuple-element.22), channel_id=1, source_target_pairs={{28,0},{30,2},{0,4},{2,6},{4,8},{6,10},{8,12},{10,14},{12,16},{14,... | collective-permute-start | bytes 2359304 | tf_op jit(solution)/shard_map/ppermute | solution.py:23
  96.8 28.0 %collective-permute-start.2 = (f32[2,512]{1,0:T(2,128)S(1)}, f32[2,512]{1,0:T(2,128)S(1)}, u32[]{:S(2)}, u32[]{:S(2)}) collective-permute-start(f32[2,512]{1,0:T(2,128)S(1)} %slice.48), channel_id=1, source_target_pairs={{4,0},{6,2},{8,4},{10,6},{12,8},{14,10},{16,12},{18,14},{20,16},{2... | collective-permute-start | bytes 12296 | tf_op jit(solution)/shard_map/ppermute | solution.py:23
  96.8 61.0 %collective-permute-start.12 = (bf16[512,768]{1,0:T(8,128)(2,1)S(1)}, bf16[512,768]{1,0:T(8,128)(2,1)S(1)}, u32[]{:S(2)}, u32[]{:S(2)}) collective-permute-start(bf16[512,768]{1,0:T(8,128)(2,1)S(1)} %get-tuple-element.21), channel_id=1, source_target_pairs={{4,0},{6,2},{8,4},{10,6},{12,8},{14,10},{16,12},{18,14},{20,16},{2... | collective-permute-start | bytes 2359304 | tf_op jit(solution)/shard_map/ppermute | solution.py:23
  108.4 49.5 %copy-start.3 = (f32[512,768]{1,0:T(8,128)S(1)}, f32[512,768]{1,0:T(8,128)}, u32[]{:S(2)}) copy-start(f32[512,768]{1,0:T(8,128)} %copy-done.2) | copy-start | bytes 4718596
  108.4 16.5 %collective-permute-start.11 = (f32[2,512]{1,0:T(2,128)S(1)}, f32[2,512]{1,0:T(2,128)S(1)}, u32[]{:S(2)}, u32[]{:S(2)}) collective-permute-start(f32[2,512]{1,0:T(2,128)S(1)} %slice.54), channel_id=1, source_target_pairs={{30,0},{0,2},{2,4},{4,6},{6,8},{8,10},{10,12},{12,14},{14,16},{16,... | collective-permute-start | bytes 12296 | tf_op jit(solution)/shard_map/ppermute | solution.py:23
  121.4 36.5 %collective-permute-start.15 = (bf16[512,768]{1,0:T(8,128)(2,1)S(1)}, bf16[512,768]{1,0:T(8,128)(2,1)S(1)}, u32[]{:S(2)}, u32[]{:S(2)}) collective-permute-start(bf16[512,768]{1,0:T(8,128)(2,1)S(1)} %get-tuple-element.24), channel_id=1, source_target_pairs={{30,0},{0,2},{2,4},{4,6},{6,8},{8,10},{10,12},{12,14},{14,16},{16,... | collective-permute-start | bytes 2359304 | tf_op jit(solution)/shard_map/ppermute | solution.py:23
  124.8 33.1 %collective-permute-start.14 = (bf16[512,768]{1,0:T(8,128)(2,1)S(1)}, bf16[512,768]{1,0:T(8,128)(2,1)S(1)}, u32[]{:S(2)}, u32[]{:S(2)}) collective-permute-start(bf16[512,768]{1,0:T(8,128)(2,1)S(1)} %get-tuple-element.23), channel_id=1, source_target_pairs={{2,0},{4,2},{6,4},{8,6},{10,8},{12,10},{14,12},{16,14},{18,16},{20... | collective-permute-start | bytes 2359304 | tf_op jit(solution)/shard_map/ppermute | solution.py:23
  124.9 32.9 %collective-permute-start.8 = (f32[2,512]{1,0:T(2,128)S(1)}, f32[2,512]{1,0:T(2,128)S(1)}, u32[]{:S(2)}, u32[]{:S(2)}) collective-permute-start(f32[2,512]{1,0:T(2,128)S(1)} %slice.52), channel_id=1, source_target_pairs={{2,0},{4,2},{6,4},{8,6},{10,8},{12,10},{14,12},{16,14},{18,16},{20... | collective-permute-start | bytes 12296 | tf_op jit(solution)/shard_map/ppermute | solution.py:23
  160.2 27.8 %all-to-all-start.1 = ((bf16[32,16,768]{2,1,0:T(8,128)(2,1)}), bf16[32,16,768]{2,1,0:T(8,128)(2,1)S(1)}, u32[]{:S(2)}, u32[]{:S(2)}) async-start(bf16[32,16,768]{2,1,0:T(8,128)(2,1)} %bitcast.26), calls=%async_computation.1 | async-start | bytes 1572864 | tf_op jit(solution)/shard_map/all_to_all | solution.py:130

commit v2 on v1

--- a/solution.py
+++ b/solution.py
@@ -1,3 +1,4 @@
+import functools
 import math
 
 import jax
@@ -85,7 +86,7 @@
     )(slots, q, *([catalog] * CAP))
 
 
-def body(left, catalog, probes, perm):
+def plain_body(left, catalog, probes, perm):
     shard_count = lax.axis_size("shard")
     rep_count = lax.axis_size("rep")
     own = lax.axis_index("shard")
@@ -134,6 +135,353 @@
     return jnp.dot(spread, arrived, preferred_element_type=jnp.float32).astype(jnp.bfloat16)
 
 
+MESH = pl.DeviceIdType.MESH
+ARRIVALS = 4
+CHUNKS = 2
+
+
+def partner_x(s):
+    return s + 1 - 2 * (s % 2)
+
+
+def partner_y(s):
+    return s + 2 - 4 * ((s // 2) % 2)
+
+
+def partner_z(s, n):
+    return (s + 4 - 8 * ((s // 2) % 2) + n) % n
+
+
+def source_z(s, n):
+    return (s - 4 + 8 * ((s // 2) % 2) + n) % n
+
+
+def is_early(s):
+    return (s % 4) * (3 - s % 4) == 0
+
+
+def attend(q, cat, slot_of):
+    slots = [slot_of(j) for j in range(CAP)]
+    picks = [jnp.maximum(slot, 0) for slot in slots]
+    scores = []
+    for j in range(CAP):
+        keys = cat[picks[j], :, :D]
+        s = lax.dot_general(q, keys, NT, preferred_element_type=jnp.float32) * SCALE
+        scores.append(jnp.where(slots[j] >= 0, s, -jnp.inf))
+    peak = scores[0]
+    for s in scores[1:]:
+        peak = jnp.maximum(peak, s)
+    peak = jnp.max(peak, axis=1, keepdims=True)
+    total = jnp.zeros_like(peak)
+    acc = None
+    for j in range(CAP):
+        e = jnp.exp(scores[j] - peak)
+        total = total + jnp.sum(e, axis=1, keepdims=True)
+        values = cat[picks[j], :, D:]
+        part = jnp.dot(e.astype(jnp.bfloat16), values, preferred_element_type=jnp.float32)
+        acc = part if acc is None else acc + part
+    lane = lax.broadcasted_iota(jnp.int32, (q.shape[0], 128), 1)
+    return acc, jnp.where(lane == 0, peak, total)
+
+
+def fused_kernel(
+    n, reps, left, cat_hbm, slots, place, pout, out,
+    cat, arr, slotv, slots_sm, accs, stats, acc_in, stat_in, own_acc, own_stat,
+    joined, gout, gin, pin,
+    cat_sem, slot_local, slot_send, slot_recv, f_send, f_recv,
+    r_send, r_recv, s_send, s_recv, p_send, p_recv, p_local, g_send, g_recv, g_local,
+):
+    count = n * reps
+    rows = left.shape[0]
+    size = rows // CHUNKS
+    each = rows // count
+    s = lax.axis_index("shard")
+    rep = lax.axis_index("rep")
+    me = s * reps + rep
+    early = is_early(s)
+    px, py, pz = partner_x(s), partner_y(s), partner_z(s, n)
+    pyz = partner_z(py, n)
+    far = jnp.where(early, partner_x(pyz), partner_x(py))
+    dests = [px, py, pyz, far]
+    zs = source_z(s, n)
+    xz = source_z(px, n)
+    origins = [px, py, partner_y(zs), jnp.where(is_early(px), partner_y(px), partner_y(xz))]
+
+    def to(shard):
+        return {"shard": shard, "rep": rep}
+
+    def device(d):
+        return {"shard": d // reps, "rep": d % reps}
+
+    def remote(src, dst, send, recv, target):
+        return pltpu.make_async_remote_copy(
+            src_ref=src, dst_ref=dst, send_sem=send, recv_sem=recv,
+            device_id=target, device_id_type=MESH,
+        )
+
+    def chunk(c):
+        return pl.ds(c * size, size)
+
+    cat_copy = pltpu.make_async_copy(cat_hbm, cat, cat_sem)
+    cat_copy.start()
+    own_slots = pltpu.make_async_copy(slots, slots_sm.at[0], slot_local.at[0])
+    own_slots.start()
+
+    barrier = pltpu.get_barrier_semaphore()
+
+    @pl.loop(1, count)
+    def _(t):
+        pl.semaphore_signal(
+            barrier, inc=1, device_id=device((me + t) % count), device_id_type=MESH
+        )
+
+    pl.semaphore_wait(barrier, count - 1)
+
+    slot_copies = [
+        remote(slots, slotv.at[a], slot_send.at[a], slot_recv.at[a], to(dests[a]))
+        for a in range(ARRIVALS)
+    ]
+    for copy in slot_copies:
+        copy.start()
+
+    def hop(src, a, c, target):
+        return remote(src, arr.at[a, chunk(c)], f_send.at[a, c], f_recv.at[a, c], to(target))
+
+    def hop_x(c):
+        return hop(left.at[chunk(c)], 0, c, px)
+
+    def hop_y(c):
+        return hop(left.at[chunk(c)], 1, c, py)
+
+    def hop_z(c):
+        return hop(arr.at[1, chunk(c)], 2, c, pz)
+
+    def hop_far(c, a):
+        return hop(arr.at[a, chunk(c)], 3, c, px)
+
+    for c in range(CHUNKS):
+        hop_y(c).start()
+        hop_x(c).start()
+
+    pos_local = pltpu.make_async_copy(pout.at[me], pin.at[me], p_local)
+    pos_local.start()
+
+    @pl.loop(1, count)
+    def _(t):
+        d = (me + t) % count
+        remote(pout.at[d], pin.at[me], p_send, p_recv, device(d)).start()
+
+    cat_copy.wait()
+    own_slots.wait()
+    for c in range(CHUNKS):
+        acc, stat = attend(left[chunk(c)], cat, lambda j: slots_sm[0, 0, j])
+        own_acc[chunk(c)] = acc
+        own_stat[chunk(c)] = stat
+
+    for a in range(ARRIVALS):
+        slot_copies[a].wait_recv()
+        local = pltpu.make_async_copy(slotv.at[a], slots_sm.at[1 + a], slot_local.at[1 + a])
+        local.start()
+        local.wait()
+
+    def back(a, c):
+        return (
+            remote(accs.at[a, chunk(c)], acc_in.at[a, chunk(c)], r_send.at[a, c],
+                   r_recv.at[a, c], to(origins[a])),
+            remote(stats.at[a, c], stat_in.at[a, c], s_send.at[a, c],
+                   s_recv.at[a, c], to(origins[a])),
+        )
+
+    def serve(a, c):
+        acc, stat = attend(arr[a, chunk(c)], cat, lambda j: slots_sm[1 + a, 1 + a, j])
+        accs[a, chunk(c)] = acc.astype(jnp.bfloat16)
+        stats[a, c] = stat.T[:8, :]
+        for copy in back(a, c):
+            copy.start()
+
+    def take_y(c):
+        hop_y(c).wait_recv()
+        hop_z(c).start()
+
+        @pl.when(early)
+        def _():
+            hop_far(c, 1).start()
+
+    def take_z(c):
+        hop_z(c).wait_recv()
+
+        @pl.when(jnp.logical_not(early))
+        def _():
+            hop_far(c, 2).start()
+
+    take_y(0)
+    serve(1, 0)
+    hop_x(0).wait_recv()
+    serve(0, 0)
+    take_y(1)
+    take_z(0)
+    serve(1, 1)
+    serve(2, 0)
+    hop_x(1).wait_recv()
+    serve(0, 1)
+    take_z(1)
+    hop_far(0, 1).wait_recv()
+    serve(3, 0)
+    serve(2, 1)
+    hop_far(1, 1).wait_recv()
+    serve(3, 1)
+
+    for c in range(CHUNKS):
+        for a in range(ARRIVALS):
+            for copy in back(a, c):
+                copy.wait_recv()
+        columns = [own_stat[chunk(c)]]
+        for a in range(ARRIVALS):
+            columns.append(jnp.concatenate([stat_in[a, c]] * 16, axis=0).T)
+        peak = columns[0][:, 0:1]
+        for column in columns[1:]:
+            peak = jnp.maximum(peak, column[:, 0:1])
+        factor = jnp.exp(columns[0][:, 0:1] - peak)
+        numer = factor * own_acc[chunk(c)]
+        denom = factor * columns[0][:, 1:2]
+        for a in range(ARRIVALS):
+            factor = jnp.exp(columns[1 + a][:, 0:1] - peak)
+            numer = numer + factor * acc_in[a, chunk(c)].astype(jnp.float32)
+            denom = denom + factor * columns[1 + a][:, 1:2]
+        joined[chunk(c)] = (numer / denom).astype(jnp.bfloat16)
+
+    index = lax.broadcasted_iota(jnp.int32, (rows, rows), 0)
+    order = jnp.where(index == place[0:1, :], 1.0, 0.0).astype(jnp.bfloat16)
+    gout[...] = jnp.dot(order, joined[...], preferred_element_type=jnp.float32).astype(jnp.bfloat16)
+
+    def lot(d):
+        return pl.ds(pl.multiple_of(d * each, each), each)
+
+    row_local = pltpu.make_async_copy(gout.at[lot(me)], gin.at[lot(me)], g_local)
+    row_local.start()
+
+    @pl.loop(1, count)
+    def _(t):
+        d = (me + t) % count
+        remote(gout.at[lot(d)], gin.at[lot(me)], g_send, g_recv, device(d)).start()
+
+    for c in range(CHUNKS):
+        for a in range(ARRIVALS):
+            for copy in back(a, c):
+                copy.wait_send()
+        hop_x(c).wait_send()
+        hop_y(c).wait_send()
+        hop_z(c).wait_send()
+        hop_far(c, 1).wait_send()
+    for copy in slot_copies:
+        copy.wait_send()
+    other = device((me + 1) % count)
+    pos = remote(pout.at[pl.ds(0, count - 1)], pin.at[pl.ds(0, count - 1)], p_send, p_recv, other)
+    pos.wait_send()
+    pos.wait_recv()
+    pos_local.wait()
+    per = 128 // each
+    groups = rows // 128
+    landing = jnp.sum(pin[...].reshape(groups, per, 8, 128), axis=1)
+    iota = lax.broadcasted_iota(jnp.int32, (rows, 128), 0)
+    spread = jnp.concatenate(
+        [jnp.where(iota == landing[g, 0:1, :], 1.0, 0.0) for g in range(groups)], axis=1
+    ).astype(jnp.bfloat16)
+
+    most = pl.ds(0, (count - 1) * each)
+    sent = remote(gout.at[most], gin.at[most], g_send, g_recv, other)
+    sent.wait_send()
+    sent.wait_recv()
+    row_local.wait()
+    out[...] = jnp.dot(spread, gin[...], preferred_element_type=jnp.float32).astype(jnp.bfloat16)
+
+
+def fused_body(left, catalog, probes, perm):
+    n = lax.axis_size("shard")
+    reps = lax.axis_size("rep")
+    s = lax.axis_index("shard")
+    me = s * reps + lax.axis_index("rep")
+    rows = left.shape[0]
+    count = n * reps
+    each = rows // count
+
+    py = partner_y(s)
+    pyz = partner_z(py, n)
+    far = jnp.where(is_early(s), partner_x(pyz), partner_x(py))
+    owners = jnp.stack([s, partner_x(s), py, pyz, far])
+    listed = probes[0]
+    hit = (listed[None, :] >= 0) & (listed[None, :] // CB_DEV == owners[:, None])
+    places = jnp.cumsum(hit.astype(jnp.int32), axis=1) - 1
+    chosen = hit[:, None, :] & (places[:, None, :] == jnp.arange(CAP)[None, :, None])
+    slots = jnp.max(jnp.where(chosen, listed[None, None, :] % CB_DEV, -1), axis=2)
+    slots = jnp.pad(slots.astype(jnp.int32), ((0, 3), (0, 128 - CAP)))
+
+    target_device = perm // rows
+    target_row = perm % rows
+    index = jnp.arange(rows)
+    earlier = (target_device[:, None] == target_device[None, :]) & (index[None, :] < index[:, None])
+    place = target_device * each + jnp.sum(earlier.astype(jnp.int32), axis=1)
+    lane = jnp.arange(128)
+    first = (me * each) % 128
+    local = lane - first
+    wanted = jnp.where((local >= 0) & (local < each), local, -rows)[None, :] + (
+        jnp.arange(count) * each
+    )[:, None]
+    pout = jnp.sum(
+        jnp.where(wanted[:, :, None] == place[None, None, :], target_row[None, None, :], 0), axis=2
+    ).astype(jnp.int32)
+    pout = jnp.broadcast_to(pout[:, None, :], (count, 8, 128))
+    place = jnp.broadcast_to(place.astype(jnp.int32)[None, :], (8, rows))
+
+    bf16, f32, i32 = jnp.bfloat16, jnp.float32, jnp.int32
+    size = rows // CHUNKS
+    dma = pltpu.SemaphoreType.DMA
+    vmem = pl.BlockSpec(memory_space=pltpu.VMEM)
+    return pl.pallas_call(
+        functools.partial(fused_kernel, n, reps),
+        out_shape=jax.ShapeDtypeStruct((rows, A), bf16),
+        in_specs=[vmem, pl.BlockSpec(memory_space=pl.ANY), vmem, vmem, vmem],
+        out_specs=vmem,
+        scratch_shapes=[
+            pltpu.VMEM((CB_DEV, BLK, D + A), bf16),
+            pltpu.VMEM((ARRIVALS, rows, D), bf16),
+            pltpu.VMEM((ARRIVALS, 8, 128), i32),
+            pltpu.SMEM((ARRIVALS + 1, 8, 128), i32),
+            pltpu.VMEM((ARRIVALS, rows, A), bf16),
+            pltpu.VMEM((ARRIVALS, CHUNKS, 8, size), f32),
+            pltpu.VMEM((ARRIVALS, rows, A), bf16),
+            pltpu.VMEM((ARRIVALS, CHUNKS, 8, size), f32),
+            pltpu.VMEM((rows, A), f32),
+            pltpu.VMEM((rows, 128), f32),
+            pltpu.VMEM((rows, A), bf16),
+            pltpu.VMEM((rows, A), bf16),
+            pltpu.VMEM((rows, A), bf16),
+            pltpu.VMEM((count, 8, 128), i32),
+            dma, dma((ARRIVALS + 1,)), dma((ARRIVALS,)), dma((ARRIVALS,)),
+            dma((ARRIVALS, CHUNKS)), dma((ARRIVALS, CHUNKS)),
+            dma((ARRIVALS, CHUNKS)), dma((ARRIVALS, CHUNKS)),
+            dma((ARRIVALS, CHUNKS)), dma((ARRIVALS, CHUNKS)),
+            dma, dma, dma, dma, dma, dma,
+        ],
+        compiler_params=pltpu.CompilerParams(
+            collective_id=0, has_side_effects=True, vmem_limit_bytes=48 * 1024 * 1024
+        ),
+        cost_estimate=pl.CostEstimate(
+            flops=10 * rows * CAP * BLK * (D + A),
+            bytes_accessed=catalog.size * 2 + rows * (D + A) * 2,
+            transcendentals=5 * rows * CAP * BLK,
+        ),
+    )(left, catalog.reshape(CB_DEV, BLK, D + A), slots, place, pout)
+
+
+def body(left, catalog, probes, perm):
+    n = lax.axis_size("shard")
+    each = left.shape[0] // (n * lax.axis_size("rep"))
+    if each % 16 == 0 and 128 % each == 0 and n % 4 == 0 and n >= 16:
+        return fused_body(left, catalog, probes, perm)
+    return plain_body(left, catalog, probes, perm)
+
+
 def solution(mesh):
     placed = (
         P(("shard", "rep"), None),

time: 191 us -> 122 us (0.64)
  the two profiles are of different devices: /device:TPU:5 before, /device:TPU:29 now
where the time goes in v2:
time: 122 us
  Pallas kernels  115 us (94%)
  other arithmetic  4.81 us (4%)
  local copies, waits for them, and re-layouts  2.21 us (2%)
    pallas_call x1, Pallas kernels, fused_body(): pl.pallas_call(functools.partial(fused_kernel, n, reps), out_shape=jax.Sh...  115 us

profile of v2, /device:TPU:29, one launch (start us, length us, event | category | flops | bytes accessed | tf_op | source)
XLA Modules:
  0.0 121.8 jit_solution(3935040498072721461)
XLA Ops:
  0.0 0.1 stack.23
  0.1 0.7 compare_bitcast_fusion
  0.8 0.7 and_select_fusion.1
  1.4 0.7 fusion.4
  2.1 0.1 fusion.5
  2.2 0.2 reduce_window_sum.11
  2.3 0.2 select_reduce_fusion.1
  2.5 0.7 add_select_fusion
  3.2 0.3 convert_reduce_fusion
  3.5 0.1 broadcast_add_fusion
  3.6 1.4 %select_reduce_fusion = s32[32,128]{1,0:T(8,128)S(1)} fusion(s32[512]{0:T(512)S(1)} %get-tuple-element.7, s32[512]{0:T(512)S(1)} %multiply_add_fusion, s32[32,128]{1,0:T(8,128)S(1)} %broadcast_add_fusion), kind=kLoop, calls=%fused_computation | loop fusion | flops 6287360 | bytes 36864 | tf_op jit(solution)/shard_map/reduce_sum | solution.py:430
  5.0 0.0 copy-start
  5.0 1.2 copy-done
  6.2 114.7 %shard_map.46 = bf16[512,768]{1,0:T(8,128)(2,1)S(1)} custom-call(bf16[512,1024]{1,0:T(8,128)(2,1)S(1)} %copy-done, bf16[8,256,1792]{2,1,0:T(8,128)(2,1)} %bitcast.12, s32[8,128]{1,0:T(8,128)S(1)} %pad.4.slots, s32[8,512]{1,0:T(8,128)S(1)} %broadcast_in_dim.34.place, s32[32,8,128]{2,1,0:T(8,128)S(1)} %broadcast_in_dim.38.pout), custom_call_target="tpu_custom_call" | custom-call | flops 11744051200 | bytes 9175040 | tf_op jit(solution)/shard_map/pallas_call | solution.py:440
  120.9 0.9 copy.6
  (7 shorter events, 0.0 us)
Async XLA Ops:
  5.0 1.2 %copy-start = (bf16[512,1024]{1,0:T(8,128)(2,1)S(1)}, bf16[512,1024]{1,0:T(8,128)(2,1)}, u32[]{:S(2)}) copy-start(bf16[512,1024]{1,0:T(8,128)(2,1)} %left.1) | copy-start | bytes 3145732

commit v3 on v2

--- a/solution.py
+++ b/solution.py
@@ -185,10 +185,10 @@
 
 
 def fused_kernel(
-    n, reps, left, cat_hbm, slots, place, pout, out,
-    cat, arr, slotv, slots_sm, accs, stats, acc_in, stat_in, own_acc, own_stat,
-    joined, gout, gin, pin,
-    cat_sem, slot_local, slot_send, slot_recv, f_send, f_recv,
+    n, reps, left_hbm, cat_hbm, slots, perm, out,
+    raw, left, pout, cat, arr, slotv, slots_sm, accs, stats, acc_in, stat_in, own_acc, own_stat,
+    joined, gin, pin,
+    left_sem, cat_sem, slot_local, slot_send, slot_recv, f_send, f_recv,
     r_send, r_recv, s_send, s_recv, p_send, p_recv, p_local, g_send, g_recv, g_local,
 ):
     count = n * reps
@@ -222,6 +222,8 @@
     def chunk(c):
         return pl.ds(c * size, size)
 
+    left_copy = pltpu.make_async_copy(left_hbm, raw, left_sem)
+    left_copy.start()
     cat_copy = pltpu.make_async_copy(cat_hbm, cat, cat_sem)
     cat_copy.start()
     own_slots = pltpu.make_async_copy(slots, slots_sm.at[0], slot_local.at[0])
@@ -234,6 +236,26 @@
         pl.semaphore_signal(
             barrier, inc=1, device_id=device((me + t) % count), device_id_type=MESH
         )
+
+    bf16, f32, i32 = jnp.bfloat16, jnp.float32, jnp.int32
+    iota = lax.broadcasted_iota
+    target = perm[...]
+    device_row = target >> (rows.bit_length() - 1)
+    row = target & (rows - 1)
+    key = (device_row & (reps - 1)) * n + (device_row >> (reps.bit_length() - 1))
+    hit = iota(i32, (count, rows), 0) == key
+    hit16 = jnp.where(hit, 1.0, 0.0).astype(bf16)
+    before = iota(i32, (rows, rows), 0) < iota(i32, (rows, rows), 1)
+    before16 = jnp.where(before, 1.0, 0.0).astype(bf16)
+    ranks = jnp.dot(hit16, before16, preferred_element_type=f32)
+    rank = jnp.sum(jnp.where(hit, ranks, 0.0), axis=0, keepdims=True)
+    place = key.astype(f32) * each + rank
+
+    left_copy.wait()
+    for c in range(CHUNKS):
+        index = (iota(i32, (size, rows), 0) + c * size).astype(f32)
+        order = jnp.where(index == place, 1.0, 0.0).astype(bf16)
+        left[chunk(c)] = jnp.dot(order, raw[...], preferred_element_type=f32).astype(bf16)
 
     pl.semaphore_wait(barrier, count - 1)
 
@@ -263,13 +285,26 @@
         hop_y(c).start()
         hop_x(c).start()
 
-    pos_local = pltpu.make_async_copy(pout.at[me], pin.at[me], p_local)
+    def key_of(d):
+        return (d % reps) * n + d // reps
+
+    shift = (me * each) % 128
+    lanes = (iota(i32, (128, rows), 0) - shift).astype(f32)
+    within = jnp.where(lanes == rank, 1.0, 0.0).astype(bf16)
+    high = jnp.where(hit, (row >> 4).astype(f32), 0.0).astype(bf16)
+    low = jnp.where(hit, (row & 15).astype(f32), 0.0).astype(bf16)
+    rows_out = 16.0 * lax.dot_general(
+        high, within, NT, preferred_element_type=f32
+    ) + lax.dot_general(low, within, NT, preferred_element_type=f32)
+    for g in range(count // 8):
+        pout[g] = rows_out[8 * g : 8 * g + 8]
+    pos_local = pltpu.make_async_copy(pout.at[key_of(me) // 8], pin.at[me], p_local)
     pos_local.start()
 
     @pl.loop(1, count)
     def _(t):
         d = (me + t) % count
-        remote(pout.at[d], pin.at[me], p_send, p_recv, device(d)).start()
+        remote(pout.at[key_of(d) // 8], pin.at[me], p_send, p_recv, device(d)).start()
 
     cat_copy.wait()
     own_slots.wait()
@@ -330,6 +365,11 @@
     serve(2, 1)
     hop_far(1, 1).wait_recv()
     serve(3, 1)
+
+    def lot(q):
+        return pl.ds(pl.multiple_of(q * each, each), each)
+
+    row_local = pltpu.make_async_copy(joined.at[lot(key_of(me))], gin.at[lot(me)], g_local)
 
     for c in range(CHUNKS):
         for a in range(ARRIVALS):
@@ -350,20 +390,23 @@
             denom = denom + factor * columns[1 + a][:, 1:2]
         joined[chunk(c)] = (numer / denom).astype(jnp.bfloat16)
 
-    index = lax.broadcasted_iota(jnp.int32, (rows, rows), 0)
-    order = jnp.where(index == place[0:1, :], 1.0, 0.0).astype(jnp.bfloat16)
-    gout[...] = jnp.dot(order, joined[...], preferred_element_type=jnp.float32).astype(jnp.bfloat16)
-
-    def lot(d):
-        return pl.ds(pl.multiple_of(d * each, each), each)
-
-    row_local = pltpu.make_async_copy(gout.at[lot(me)], gin.at[lot(me)], g_local)
-    row_local.start()
-
-    @pl.loop(1, count)
-    def _(t):
-        d = (me + t) % count
-        remote(gout.at[lot(d)], gin.at[lot(me)], g_send, g_recv, device(d)).start()
+        def row_copy(shard):
+            return remote(
+                joined.at[lot(c * n + shard)], gin.at[lot(me)], g_send, g_recv,
+                {"shard": shard, "rep": c},
+            )
+
+        @pl.when(rep != c)
+        def _():
+            row_copy(s).start()
+
+        @pl.when(rep == c)
+        def _():
+            row_local.start()
+
+        @pl.loop(1, n)
+        def _(t):
+            row_copy((s + t) % n).start()
 
     for c in range(CHUNKS):
         for a in range(ARRIVALS):
@@ -376,20 +419,26 @@
     for copy in slot_copies:
         copy.wait_send()
     other = device((me + 1) % count)
-    pos = remote(pout.at[pl.ds(0, count - 1)], pin.at[pl.ds(0, count - 1)], p_send, p_recv, other)
+    tiles = pin.at[pl.ds(0, count - 1)]
+    pos = remote(tiles, tiles, p_send, p_recv, other)
     pos.wait_send()
     pos.wait_recv()
     pos_local.wait()
     per = 128 // each
     groups = rows // 128
-    landing = jnp.sum(pin[...].reshape(groups, per, 8, 128), axis=1)
-    iota = lax.broadcasted_iota(jnp.int32, (rows, 128), 0)
-    spread = jnp.concatenate(
-        [jnp.where(iota == landing[g, 0:1, :], 1.0, 0.0) for g in range(groups)], axis=1
-    ).astype(jnp.bfloat16)
+    mine = iota(i32, (8, 128), 0) == key_of(me) % 8
+    landing_row = iota(i32, (rows, 128), 0).astype(f32)
+    spread = []
+    for g in range(groups):
+        tile = pin[g * per]
+        for b in range(1, per):
+            tile = tile + pin[g * per + b]
+        landing = jnp.sum(jnp.where(mine, tile, 0.0), axis=0, keepdims=True)
+        spread.append(jnp.where(landing_row == landing, 1.0, 0.0))
+    spread = jnp.concatenate(spread, axis=1).astype(bf16)
 
     most = pl.ds(0, (count - 1) * each)
-    sent = remote(gout.at[most], gin.at[most], g_send, g_recv, other)
+    sent = remote(joined.at[most], gin.at[most], g_send, g_recv, other)
     sent.wait_send()
     sent.wait_recv()
     row_local.wait()
@@ -400,10 +449,8 @@
     n = lax.axis_size("shard")
     reps = lax.axis_size("rep")
     s = lax.axis_index("shard")
-    me = s * reps + lax.axis_index("rep")
     rows = left.shape[0]
     count = n * reps
-    each = rows // count
 
     py = partner_y(s)
     pyz = partner_z(py, n)
@@ -416,23 +463,6 @@
     slots = jnp.max(jnp.where(chosen, listed[None, None, :] % CB_DEV, -1), axis=2)
     slots = jnp.pad(slots.astype(jnp.int32), ((0, 3), (0, 128 - CAP)))
 
-    target_device = perm // rows
-    target_row = perm % rows
-    index = jnp.arange(rows)
-    earlier = (target_device[:, None] == target_device[None, :]) & (index[None, :] < index[:, None])
-    place = target_device * each + jnp.sum(earlier.astype(jnp.int32), axis=1)
-    lane = jnp.arange(128)
-    first = (me * each) % 128
-    local = lane - first
-    wanted = jnp.where((local >= 0) & (local < each), local, -rows)[None, :] + (
-        jnp.arange(count) * each
-    )[:, None]
-    pout = jnp.sum(
-        jnp.where(wanted[:, :, None] == place[None, None, :], target_row[None, None, :], 0), axis=2
-    ).astype(jnp.int32)
-    pout = jnp.broadcast_to(pout[:, None, :], (count, 8, 128))
-    place = jnp.broadcast_to(place.astype(jnp.int32)[None, :], (8, rows))
-
     bf16, f32, i32 = jnp.bfloat16, jnp.float32, jnp.int32
     size = rows // CHUNKS
     dma = pltpu.SemaphoreType.DMA
@@ -440,9 +470,12 @@
     return pl.pallas_call(
         functools.partial(fused_kernel, n, reps),
         out_shape=jax.ShapeDtypeStruct((rows, A), bf16),
-        in_specs=[vmem, pl.BlockSpec(memory_space=pl.ANY), vmem, vmem, vmem],
+        in_specs=[pl.BlockSpec(memory_space=pl.ANY)] * 2 + [vmem, vmem],
         out_specs=vmem,
         scratch_shapes=[
+            pltpu.VMEM((rows, D), bf16),
+            pltpu.VMEM((rows, D), bf16),
+            pltpu.VMEM((count // 8, 8, 128), f32),
             pltpu.VMEM((CB_DEV, BLK, D + A), bf16),
             pltpu.VMEM((ARRIVALS, rows, D), bf16),
             pltpu.VMEM((ARRIVALS, 8, 128), i32),
@@ -455,9 +488,8 @@
             pltpu.VMEM((rows, 128), f32),
             pltpu.VMEM((rows, A), bf16),
             pltpu.VMEM((rows, A), bf16),
-            pltpu.VMEM((rows, A), bf16),
-            pltpu.VMEM((count, 8, 128), i32),
-            dma, dma((ARRIVALS + 1,)), dma((ARRIVALS,)), dma((ARRIVALS,)),
+            pltpu.VMEM((count, 8, 128), f32),
+            dma, dma, dma((ARRIVALS + 1,)), dma((ARRIVALS,)), dma((ARRIVALS,)),
             dma((ARRIVALS, CHUNKS)), dma((ARRIVALS, CHUNKS)),
             dma((ARRIVALS, CHUNKS)), dma((ARRIVALS, CHUNKS)),
             dma((ARRIVALS, CHUNKS)), dma((ARRIVALS, CHUNKS)),
@@ -471,13 +503,15 @@
             bytes_accessed=catalog.size * 2 + rows * (D + A) * 2,
             transcendentals=5 * rows * CAP * BLK,
         ),
-    )(left, catalog.reshape(CB_DEV, BLK, D + A), slots, place, pout)
+    )(left, catalog.reshape(CB_DEV, BLK, D + A), slots, perm.reshape(1, rows))
 
 
 def body(left, catalog, probes, perm):
     n = lax.axis_size("shard")
-    each = left.shape[0] // (n * lax.axis_size("rep"))
-    if each % 16 == 0 and 128 % each == 0 and n % 4 == 0 and n >= 16:
+    reps = lax.axis_size("rep")
+    rows = left.shape[0]
+    each = rows // (n * reps)
+    if each == 16 and rows & (rows - 1) == 0 and reps == CHUNKS and n % 4 == 0 and n >= 16:
         return fused_body(left, catalog, probes, perm)
     return plain_body(left, catalog, probes, perm)
 

time: 122 us -> 115 us (0.943)
  the two profiles are of different devices: /device:TPU:29 before, /device:TPU:5 now
where the time goes in v3:
time: 115 us; the launch traced here: 113 us
  Pallas kernels  108 us (94%)
  local copies, waits for them, and re-layouts  2.87 us (2%)
  other arithmetic  2.42 us (2%)
    pallas_call x1, Pallas kernels, fused_body(): pl.pallas_call(functools.partial(fused_kernel, n, reps), out_shape=jax.Sh...  108 us
    unnamed x5, local copies, waits for them, and re-layouts  2.78 us

profile of v3, /device:TPU:5, one launch (start us, length us, event | category | flops | bytes accessed | tf_op | source)
XLA Modules:
  0.0 113.3 jit_solution(7782366274354416361)
XLA Ops:
  0.0 0.1 stack.23
  0.1 0.7 compare_bitcast_fusion
  0.7 0.7 and_select_fusion
  1.4 0.7 fusion.2
  2.1 0.1 fusion.3
  2.1 0.2 reduce_window_sum.11
  2.3 0.2 select_reduce_fusion
  2.5 0.0 copy-start
  2.5 1.2 %copy-done = bf16[512,1024]{1,0:T(8,128)(2,1)S(1)} copy-done((bf16[512,1024]{1,0:T(8,128)(2,1)S(1)}, bf16[512,1024]{1,0:T(8,128)(2,1)}, u32[]{:S(2)}) %copy-start) | copy-done | bytes 1048600
  3.8 0.0 copy-start.1
  3.8 0.7 copy-done.1
  4.4 107.9 %shard_map.46 = bf16[512,768]{1,0:T(8,128)(2,1)S(1)} custom-call(bf16[512,1024]{1,0:T(8,128)(2,1)S(1)} %copy-done, bf16[8,256,1792]{2,1,0:T(8,128)(2,1)} %bitcast.14, s32[8,128]{1,0:T(8,128)S(1)} %pad.4.slots, s32[1,512]{1,0:T(1,128)S(1)} %bitcast.13), custom_call_target="tpu_custom_call" | custom-call | flops 11744051200 | bytes 9175040 | tf_op jit(solution)/shard_map/pallas_call | solution.py:470
  112.4 0.9 copy.6
  (2 shorter events, 0.0 us)
Async XLA Ops:
  2.5 1.2 %copy-start = (bf16[512,1024]{1,0:T(8,128)(2,1)S(1)}, bf16[512,1024]{1,0:T(8,128)(2,1)}, u32[]{:S(2)}) copy-start(bf16[512,1024]{1,0:T(8,128)(2,1)} %left_hbm.1) | copy-start | bytes 3145732
  3.8 0.7 copy-start.1

commit v4 on v3

--- a/solution.py
+++ b/solution.py
@@ -137,7 +137,7 @@
 
 MESH = pl.DeviceIdType.MESH
 ARRIVALS = 4
-CHUNKS = 2
+CHUNKS = 4
 
 
 def partner_x(s):
@@ -154,6 +154,14 @@
 
 def source_z(s, n):
     return (s - 4 + 8 * ((s // 2) % 2) + n) % n
+
+
+def parity(s):
+    return (s + s // 2 + s // 4) % 2
+
+
+def of_parity(u, p):
+    return 2 * u + (p + u + u // 2) % 2
 
 
 def is_early(s):
@@ -242,7 +250,9 @@
     target = perm[...]
     device_row = target >> (rows.bit_length() - 1)
     row = target & (rows - 1)
-    key = (device_row & (reps - 1)) * n + (device_row >> (reps.bit_length() - 1))
+    shard_row = device_row >> (reps.bit_length() - 1)
+    side = (shard_row + (shard_row >> 1) + (shard_row >> 2)) & 1
+    key = (device_row & (reps - 1)) * n + side * (n // 2) + (shard_row >> 1)
     hit = iota(i32, (count, rows), 0) == key
     hit16 = jnp.where(hit, 1.0, 0.0).astype(bf16)
     before = iota(i32, (rows, rows), 0) < iota(i32, (rows, rows), 1)
@@ -286,7 +296,8 @@
         hop_x(c).start()
 
     def key_of(d):
-        return (d % reps) * n + d // reps
+        shard = d // reps
+        return (d % reps) * n + parity(shard) * (n // 2) + shard // 2
 
     shift = (me * each) % 128
     lanes = (iota(i32, (128, rows), 0) - shift).astype(f32)
@@ -331,6 +342,8 @@
         acc, stat = attend(arr[a, chunk(c)], cat, lambda j: slots_sm[1 + a, 1 + a, j])
         accs[a, chunk(c)] = acc.astype(jnp.bfloat16)
         stats[a, c] = stat.T[:8, :]
+
+    def give(a, c):
         for copy in back(a, c):
             copy.start()
 
@@ -349,22 +362,26 @@
         def _():
             hop_far(c, 2).start()
 
-    take_y(0)
-    serve(1, 0)
-    hop_x(0).wait_recv()
-    serve(0, 0)
-    take_y(1)
-    take_z(0)
-    serve(1, 1)
-    serve(2, 0)
-    hop_x(1).wait_recv()
-    serve(0, 1)
-    take_z(1)
-    hop_far(0, 1).wait_recv()
-    serve(3, 0)
-    serve(2, 1)
-    hop_far(1, 1).wait_recv()
-    serve(3, 1)
+    for c in range(CHUNKS):
+        take_y(c)
+        if c > 0:
+            take_z(c - 1)
+        serve(1, c)
+        give(1, c)
+        hop_x(c).wait_recv()
+        serve(0, c)
+        if c > 0:
+            serve(2, c - 1)
+            give(2, c - 1)
+    last = CHUNKS - 1
+    take_z(last)
+    serve(2, last)
+    give(2, last)
+    for c in range(CHUNKS):
+        hop_far(c, 1).wait_recv()
+        serve(3, c)
+        give(3, c)
+        give(0, c)
 
     def lot(q):
         return pl.ds(pl.multiple_of(q * each, each), each)
@@ -390,23 +407,27 @@
             denom = denom + factor * columns[1 + a][:, 1:2]
         joined[chunk(c)] = (numer / denom).astype(jnp.bfloat16)
 
-        def row_copy(shard):
+        half = n // 2
+        here = (rep - c // 2) * (rep - c // 2) + (parity(s) - c % 2) * (parity(s) - c % 2) == 0
+
+        def row_copy(t):
+            u = (s // 2 + t) % half
             return remote(
-                joined.at[lot(c * n + shard)], gin.at[lot(me)], g_send, g_recv,
-                {"shard": shard, "rep": c},
+                joined.at[lot(c * half + u)], gin.at[lot(me)], g_send, g_recv,
+                {"shard": of_parity(u, c % 2), "rep": c // 2},
             )
 
-        @pl.when(rep != c)
+        @pl.when(jnp.logical_not(here))
         def _():
-            row_copy(s).start()
-
-        @pl.when(rep == c)
+            row_copy(0).start()
+
+        @pl.when(here)
         def _():
             row_local.start()
 
-        @pl.loop(1, n)
+        @pl.loop(1, half)
         def _(t):
-            row_copy((s + t) % n).start()
+            row_copy(t).start()
 
     for c in range(CHUNKS):
         for a in range(ARRIVALS):
@@ -496,7 +517,7 @@
             dma, dma, dma, dma, dma, dma,
         ],
         compiler_params=pltpu.CompilerParams(
-            collective_id=0, has_side_effects=True, vmem_limit_bytes=48 * 1024 * 1024
+            collective_id=0, has_side_effects=True, vmem_limit_bytes=60 * 1024 * 1024
         ),
         cost_estimate=pl.CostEstimate(
             flops=10 * rows * CAP * BLK * (D + A),
@@ -511,7 +532,7 @@
     reps = lax.axis_size("rep")
     rows = left.shape[0]
     each = rows // (n * reps)
-    if each == 16 and rows & (rows - 1) == 0 and reps == CHUNKS and n % 4 == 0 and n >= 16:
+    if each == 16 and rows & (rows - 1) == 0 and 2 * reps == CHUNKS and n % 4 == 0 and n >= 16:
         return fused_body(left, catalog, probes, perm)
     return plain_body(left, catalog, probes, perm)
 

time: 115 us -> 112 us (0.974); the launches traced: 113 us -> 112 us
  Pallas kernels: 108 us -> 106 us
    pallas_call x1, Pallas kernels: 108 us -> 106 us  [fused_body(): pl.pallas_call(functools.partial(fused_kernel, n, reps), out_shape=jax.Sh...]
    unnamed x5 -> x1, local copies, waits for them, and re-layouts: 2.78 us -> 2.06 us
where the time goes in v4:
time: 112 us
  Pallas kernels  106 us (95%)
  local copies, waits for them, and re-layouts  2.75 us (2%)
  other arithmetic  2.42 us (2%)
    pallas_call x1, Pallas kernels, fused_body(): pl.pallas_call(functools.partial(fused_kernel, n, reps), out_shape=jax.Sh...  106 us

profile of v4, /device:TPU:5, one launch (start us, length us, event | category | flops | bytes accessed | tf_op | source)
XLA Modules:
  0.0 111.7 jit_solution(1599455578535557271)
XLA Ops:
  0.0 0.1 stack.23
  0.1 0.7 compare_bitcast_fusion
  0.7 0.7 and_select_fusion
  1.4 0.7 fusion.2
  2.1 0.1 fusion.3
  2.1 0.2 reduce_window_sum.11
  2.3 0.2 select_reduce_fusion
  2.5 0.6 pad.4.slots
  3.1 106.5 %shard_map.46 = bf16[512,768]{1,0:T(8,128)(2,1)} custom-call(bf16[512,1024]{1,0:T(8,128)(2,1)} %left_hbm.1, bf16[8,256,1792]{2,1,0:T(8,128)(2,1)} %bitcast.13, s32[8,128]{1,0:T(8,128)} %pad.4.slots, s32[1,512]{1,0:T(1,128)} %bitcast.14), custom_call_target="tpu_custom_call" | custom-call | flops 11744051200 | bytes 9175040 | tf_op jit(solution)/shard_map/pallas_call | solution.py:491
  109.6 2.1 %copy.6 = bf16[512,768]{1,0:T(8,128)(2,1)} copy(bf16[512,768]{1,0:T(8,128)(2,1)} %shard_map.46) | data formatting | bytes 1572864
  (1 shorter events, 0.0 us)

commit v5 on v4

--- a/solution.py
+++ b/solution.py
@@ -213,7 +213,9 @@
     dests = [px, py, pyz, far]
     zs = source_z(s, n)
     xz = source_z(px, n)
-    origins = [px, py, partner_y(zs), jnp.where(is_early(px), partner_y(px), partner_y(xz))]
+    pfar = (s + 2 - 4 * (s % 2) + n) % n
+    meets = [partner_y(px), py, zs, jnp.where(is_early(px), px, xz)]
+    source = py * reps + rep
 
     def to(shard):
         return {"shard": shard, "rep": rep}
@@ -288,8 +290,8 @@
     def hop_z(c):
         return hop(arr.at[1, chunk(c)], 2, c, pz)
 
-    def hop_far(c, a):
-        return hop(arr.at[a, chunk(c)], 3, c, px)
+    def hop_far(c, a, target):
+        return hop(arr.at[a, chunk(c)], 3, c, target)
 
     for c in range(CHUNKS):
         hop_y(c).start()
@@ -317,12 +319,22 @@
         d = (me + t) % count
         remote(pout.at[key_of(d) // 8], pin.at[me], p_send, p_recv, device(d)).start()
 
+    def back(a, c):
+        return (
+            remote(accs.at[a, chunk(c)], acc_in.at[a, chunk(c)], r_send.at[a, c],
+                   r_recv.at[a, c], to(meets[a])),
+            remote(stats.at[a, c], stat_in.at[a, c], s_send.at[a, c],
+                   s_recv.at[a, c], to(meets[a])),
+        )
+
+    def send_off(a, c, acc, stat):
+        accs[a, chunk(c)] = acc.astype(jnp.bfloat16)
+        stats[a, c] = stat.T[:8, :]
+
     cat_copy.wait()
     own_slots.wait()
     for c in range(CHUNKS):
-        acc, stat = attend(left[chunk(c)], cat, lambda j: slots_sm[0, 0, j])
-        own_acc[chunk(c)] = acc
-        own_stat[chunk(c)] = stat
+        send_off(1, c, *attend(left[chunk(c)], cat, lambda j: slots_sm[0, 0, j]))
 
     for a in range(ARRIVALS):
         slot_copies[a].wait_recv()
@@ -330,45 +342,49 @@
         local.start()
         local.wait()
 
-    def back(a, c):
-        return (
-            remote(accs.at[a, chunk(c)], acc_in.at[a, chunk(c)], r_send.at[a, c],
-                   r_recv.at[a, c], to(origins[a])),
-            remote(stats.at[a, c], stat_in.at[a, c], s_send.at[a, c],
-                   s_recv.at[a, c], to(origins[a])),
-        )
-
     def serve(a, c):
         acc, stat = attend(arr[a, chunk(c)], cat, lambda j: slots_sm[1 + a, 1 + a, j])
-        accs[a, chunk(c)] = acc.astype(jnp.bfloat16)
-        stats[a, c] = stat.T[:8, :]
+        if a == 1:
+            own_acc[chunk(c)] = acc
+            own_stat[chunk(c)] = stat
+        else:
+            send_off(a, c, acc, stat)
 
     def give(a, c):
         for copy in back(a, c):
             copy.start()
 
+    def by_x(c):
+        return c % 2 == 0
+
     def take_y(c):
         hop_y(c).wait_recv()
         hop_z(c).start()
-
-        @pl.when(early)
-        def _():
-            hop_far(c, 1).start()
+        if by_x(c):
+
+            @pl.when(early)
+            def _():
+                hop_far(c, 1, px).start()
+
+    def take_x(c):
+        hop_x(c).wait_recv()
+        if not by_x(c):
+            hop_far(c, 0, pfar).start()
 
     def take_z(c):
         hop_z(c).wait_recv()
-
-        @pl.when(jnp.logical_not(early))
-        def _():
-            hop_far(c, 2).start()
+        if by_x(c):
+
+            @pl.when(jnp.logical_not(early))
+            def _():
+                hop_far(c, 2, px).start()
 
     for c in range(CHUNKS):
         take_y(c)
+        take_x(c)
         if c > 0:
             take_z(c - 1)
         serve(1, c)
-        give(1, c)
-        hop_x(c).wait_recv()
         serve(0, c)
         if c > 0:
             serve(2, c - 1)
@@ -378,15 +394,16 @@
     serve(2, last)
     give(2, last)
     for c in range(CHUNKS):
-        hop_far(c, 1).wait_recv()
+        hop_far(c, 1, px).wait_recv()
         serve(3, c)
         give(3, c)
         give(0, c)
+        give(1, c)
 
     def lot(q):
         return pl.ds(pl.multiple_of(q * each, each), each)
 
-    row_local = pltpu.make_async_copy(joined.at[lot(key_of(me))], gin.at[lot(me)], g_local)
+    row_local = pltpu.make_async_copy(joined.at[lot(key_of(me))], gin.at[lot(source)], g_local)
 
     for c in range(CHUNKS):
         for a in range(ARRIVALS):
@@ -413,7 +430,7 @@
         def row_copy(t):
             u = (s // 2 + t) % half
             return remote(
-                joined.at[lot(c * half + u)], gin.at[lot(me)], g_send, g_recv,
+                joined.at[lot(c * half + u)], gin.at[lot(source)], g_send, g_recv,
                 {"shard": of_parity(u, c % 2), "rep": c // 2},
             )
 
@@ -436,7 +453,7 @@
         hop_x(c).wait_send()
         hop_y(c).wait_send()
         hop_z(c).wait_send()
-        hop_far(c, 1).wait_send()
+        hop_far(c, 1, px).wait_send()
     for copy in slot_copies:
         copy.wait_send()
     other = device((me + 1) % count)

time: 112 us -> 114 us (1.018)
  Pallas kernels: 106 us -> 108 us
    pallas_call x1, Pallas kernels: 106 us -> 108 us  [fused_body(): pl.pallas_call(functools.partial(fused_kernel, n, reps), out_shape=jax.Sh...]
where the time goes in v5:
time: 114 us; the launch traced here: 113 us
  Pallas kernels  108 us (95%)
  local copies, waits for them, and re-layouts  2.75 us (2%)
  other arithmetic  2.42 us (2%)
    pallas_call x1, Pallas kernels, fused_body(): pl.pallas_call(functools.partial(fused_kernel, n, reps), out_shape=jax.Sh...  108 us

profile of v5, /device:TPU:5, one launch (start us, length us, event | category | flops | bytes accessed | tf_op | source)
XLA Modules:
  0.0 113.3 jit_solution(483157028700817980)
XLA Ops:
  0.0 0.1 stack.23
  0.1 0.7 compare_bitcast_fusion
  0.7 0.7 and_select_fusion
  1.4 0.7 fusion.2
  2.1 0.1 fusion.3
  2.1 0.2 reduce_window_sum.11
  2.3 0.2 select_reduce_fusion
  2.5 0.6 pad.4.slots
  3.1 108.2 %shard_map.46 = bf16[512,768]{1,0:T(8,128)(2,1)} custom-call(bf16[512,1024]{1,0:T(8,128)(2,1)} %left_hbm.1, bf16[8,256,1792]{2,1,0:T(8,128)(2,1)} %bitcast.13, s32[8,128]{1,0:T(8,128)} %pad.4.slots, s32[1,512]{1,0:T(1,128)} %bitcast.14), custom_call_target="tpu_custom_call" | custom-call | flops 11744051200 | bytes 9175040 | tf_op jit(solution)/shard_map/pallas_call | solution.py:508
  111.3 2.1 %copy.6 = bf16[512,768]{1,0:T(8,128)(2,1)} copy(bf16[512,768]{1,0:T(8,128)(2,1)} %shard_map.46) | data formatting | bytes 1572864
  (1 shorter events, 0.0 us)

commit v6 on v5

--- a/solution.py
+++ b/solution.py
@@ -138,6 +138,7 @@
 MESH = pl.DeviceIdType.MESH
 ARRIVALS = 4
 CHUNKS = 4
+UNITS = 2
 
 
 def partner_x(s):
@@ -234,6 +235,9 @@
 
     left_copy = pltpu.make_async_copy(left_hbm, raw, left_sem)
     left_copy.start()
+    def unit(u):
+        return pl.ds(u * (rows // UNITS), rows // UNITS)
+
     cat_copy = pltpu.make_async_copy(cat_hbm, cat, cat_sem)
     cat_copy.start()
     own_slots = pltpu.make_async_copy(slots, slots_sm.at[0], slot_local.at[0])
@@ -319,22 +323,22 @@
         d = (me + t) % count
         remote(pout.at[key_of(d) // 8], pin.at[me], p_send, p_recv, device(d)).start()
 
-    def back(a, c):
+    def back(a, u):
         return (
-            remote(accs.at[a, chunk(c)], acc_in.at[a, chunk(c)], r_send.at[a, c],
-                   r_recv.at[a, c], to(meets[a])),
-            remote(stats.at[a, c], stat_in.at[a, c], s_send.at[a, c],
-                   s_recv.at[a, c], to(meets[a])),
+            remote(accs.at[a, unit(u)], acc_in.at[a, unit(u)], r_send.at[a, u],
+                   r_recv.at[a, u], to(meets[a])),
+            remote(stats.at[a, u], stat_in.at[a, u], s_send.at[a, u],
+                   s_recv.at[a, u], to(meets[a])),
         )
 
-    def send_off(a, c, acc, stat):
-        accs[a, chunk(c)] = acc.astype(jnp.bfloat16)
-        stats[a, c] = stat.T[:8, :]
+    def send_off(a, u, acc, stat):
+        accs[a, unit(u)] = acc.astype(jnp.bfloat16)
+        stats[a, u] = stat.T[:8, :]
 
     cat_copy.wait()
     own_slots.wait()
-    for c in range(CHUNKS):
-        send_off(1, c, *attend(left[chunk(c)], cat, lambda j: slots_sm[0, 0, j]))
+    for u in range(UNITS):
+        send_off(1, u, *attend(left[unit(u)], cat, lambda j: slots_sm[0, 0, j]))
 
     for a in range(ARRIVALS):
         slot_copies[a].wait_recv()
@@ -342,16 +346,16 @@
         local.start()
         local.wait()
 
-    def serve(a, c):
-        acc, stat = attend(arr[a, chunk(c)], cat, lambda j: slots_sm[1 + a, 1 + a, j])
+    def serve(a, u):
+        acc, stat = attend(arr[a, unit(u)], cat, lambda j: slots_sm[1 + a, 1 + a, j])
         if a == 1:
-            own_acc[chunk(c)] = acc
-            own_stat[chunk(c)] = stat
+            own_acc[unit(u)] = acc
+            own_stat[unit(u)] = stat
         else:
-            send_off(a, c, acc, stat)
-
-    def give(a, c):
-        for copy in back(a, c):
+            send_off(a, u, acc, stat)
+
+    def give(a, u):
+        for copy in back(a, u):
             copy.start()
 
     def by_x(c):
@@ -379,26 +383,37 @@
             def _():
                 hop_far(c, 2, px).start()
 
-    for c in range(CHUNKS):
-        take_y(c)
-        take_x(c)
-        if c > 0:
-            take_z(c - 1)
-        serve(1, c)
-        serve(0, c)
-        if c > 0:
-            serve(2, c - 1)
-            give(2, c - 1)
-    last = CHUNKS - 1
-    take_z(last)
-    serve(2, last)
-    give(2, last)
-    for c in range(CHUNKS):
-        hop_far(c, 1, px).wait_recv()
-        serve(3, c)
-        give(3, c)
-        give(0, c)
-        give(1, c)
+    take_y(0)
+    take_x(0)
+    take_y(1)
+    take_x(1)
+    take_z(0)
+    serve(1, 0)
+    take_y(2)
+    take_z(1)
+    take_x(2)
+    serve(0, 0)
+    take_y(3)
+    take_z(2)
+    take_x(3)
+    serve(2, 0)
+    give(2, 0)
+    take_z(3)
+    give(1, 0)
+    give(0, 0)
+    serve(1, 1)
+    serve(0, 1)
+    serve(2, 1)
+    give(2, 1)
+    per_unit = CHUNKS // UNITS
+    for u in range(UNITS):
+        for c in range(u * per_unit, (u + 1) * per_unit):
+            hop_far(c, 1, px).wait_recv()
+        serve(3, u)
+        give(3, u)
+        if u == 0:
+            give(1, 1)
+            give(0, 1)
 
     def lot(q):
         return pl.ds(pl.multiple_of(q * each, each), each)
@@ -406,12 +421,15 @@
     row_local = pltpu.make_async_copy(joined.at[lot(key_of(me))], gin.at[lot(source)], g_local)
 
     for c in range(CHUNKS):
-        for a in range(ARRIVALS):
-            for copy in back(a, c):
-                copy.wait_recv()
+        u = c // per_unit
+        part = pl.ds(c % per_unit * size, size)
+        if c % per_unit == 0:
+            for a in range(ARRIVALS):
+                for copy in back(a, u):
+                    copy.wait_recv()
         columns = [own_stat[chunk(c)]]
         for a in range(ARRIVALS):
-            columns.append(jnp.concatenate([stat_in[a, c]] * 16, axis=0).T)
+            columns.append(jnp.concatenate([stat_in[a, u, :, part]] * 16, axis=0).T)
         peak = columns[0][:, 0:1]
         for column in columns[1:]:
             peak = jnp.maximum(peak, column[:, 0:1])
@@ -428,10 +446,10 @@
         here = (rep - c // 2) * (rep - c // 2) + (parity(s) - c % 2) * (parity(s) - c % 2) == 0
 
         def row_copy(t):
-            u = (s // 2 + t) % half
+            v = (s // 2 + t) % half
             return remote(
-                joined.at[lot(c * half + u)], gin.at[lot(source)], g_send, g_recv,
-                {"shard": of_parity(u, c % 2), "rep": c // 2},
+                joined.at[lot(c * half + v)], gin.at[lot(source)], g_send, g_recv,
+                {"shard": of_parity(v, c % 2), "rep": c // 2},
             )
 
         @pl.when(jnp.logical_not(here))
@@ -446,10 +464,11 @@
         def _(t):
             row_copy(t).start()
 
+    for u in range(UNITS):
+        for a in range(ARRIVALS):
+            for copy in back(a, u):
+                copy.wait_send()
     for c in range(CHUNKS):
-        for a in range(ARRIVALS):
-            for copy in back(a, c):
-                copy.wait_send()
         hop_x(c).wait_send()
         hop_y(c).wait_send()
         hop_z(c).wait_send()
@@ -519,9 +538,9 @@
             pltpu.VMEM((ARRIVALS, 8, 128), i32),
             pltpu.SMEM((ARRIVALS + 1, 8, 128), i32),
             pltpu.VMEM((ARRIVALS, rows, A), bf16),
-            pltpu.VMEM((ARRIVALS, CHUNKS, 8, size), f32),
+            pltpu.VMEM((ARRIVALS, UNITS, 8, rows // UNITS), f32),
             pltpu.VMEM((ARRIVALS, rows, A), bf16),
-            pltpu.VMEM((ARRIVALS, CHUNKS, 8, size), f32),
+            pltpu.VMEM((ARRIVALS, UNITS, 8, rows // UNITS), f32),
             pltpu.VMEM((rows, A), f32),
             pltpu.VMEM((rows, 128), f32),
             pltpu.VMEM((rows, A), bf16),
@@ -529,8 +548,8 @@
             pltpu.VMEM((count, 8, 128), f32),
             dma, dma, dma((ARRIVALS + 1,)), dma((ARRIVALS,)), dma((ARRIVALS,)),
             dma((ARRIVALS, CHUNKS)), dma((ARRIVALS, CHUNKS)),
-            dma((ARRIVALS, CHUNKS)), dma((ARRIVALS, CHUNKS)),
-            dma((ARRIVALS, CHUNKS)), dma((ARRIVALS, CHUNKS)),
+            dma((ARRIVALS, UNITS)), dma((ARRIVALS, UNITS)),
+            dma((ARRIVALS, UNITS)), dma((ARRIVALS, UNITS)),
             dma, dma, dma, dma, dma, dma,
         ],
         compiler_params=pltpu.CompilerParams(

time: 114 us -> 108 us (0.947)
  Pallas kernels: 108 us -> 102 us
    pallas_call x1, Pallas kernels: 108 us -> 102 us  [fused_body(): pl.pallas_call(functools.partial(fused_kernel, n, reps), out_shape=jax.Sh...]
where the time goes in v6:
time: 108 us
  Pallas kernels  102 us (94%)
  local copies, waits for them, and re-layouts  2.75 us (3%)
  other arithmetic  2.42 us (2%)
    pallas_call x1, Pallas kernels, fused_body(): pl.pallas_call(functools.partial(fused_kernel, n, reps), out_shape=jax.Sh...  102 us

profile of v6, /device:TPU:5, one launch (start us, length us, event | category | flops | bytes accessed | tf_op | source)
XLA Modules:
  0.0 107.6 jit_solution(8495698619166177965)
XLA Ops:
  0.0 0.1 stack.23
  0.1 0.7 compare_bitcast_fusion
  0.7 0.7 and_select_fusion
  1.4 0.7 fusion.2
  2.1 0.1 fusion.3
  2.1 0.2 reduce_window_sum.11
  2.3 0.2 select_reduce_fusion
  2.5 0.6 pad.4.slots
  3.1 102.4 %shard_map.46 = bf16[512,768]{1,0:T(8,128)(2,1)} custom-call(bf16[512,1024]{1,0:T(8,128)(2,1)} %left_hbm.1, bf16[8,256,1792]{2,1,0:T(8,128)(2,1)} %bitcast.13, s32[8,128]{1,0:T(8,128)} %pad.4.slots, s32[1,512]{1,0:T(1,128)} %bitcast.14), custom_call_target="tpu_custom_call" | custom-call | flops 11744051200 | bytes 9175040 | tf_op jit(solution)/shard_map/pallas_call | solution.py:527
  105.5 2.1 %copy.6 = bf16[512,768]{1,0:T(8,128)(2,1)} copy(bf16[512,768]{1,0:T(8,128)(2,1)} %shard_map.46) | data formatting | bytes 1572864
  (1 shorter events, 0.0 us)

commit v7 on v6

--- a/solution.py
+++ b/solution.py
@@ -297,9 +297,14 @@
     def hop_far(c, a, target):
         return hop(arr.at[a, chunk(c)], 3, c, target)
 
-    for c in range(CHUNKS):
+    def launch(c):
+        if c > 0:
+            hop_y(c - 1).wait_send()
+            hop_x(c - 1).wait_send()
         hop_y(c).start()
         hop_x(c).start()
+
+    launch(0)
 
     def key_of(d):
         shard = d // reps
@@ -339,6 +344,8 @@
     own_slots.wait()
     for u in range(UNITS):
         send_off(1, u, *attend(left[unit(u)], cat, lambda j: slots_sm[0, 0, j]))
+        if u == 0:
+            launch(1)
 
     for a in range(ARRIVALS):
         slot_copies[a].wait_recv()
@@ -385,16 +392,18 @@
 
     take_y(0)
     take_x(0)
+    launch(2)
+    take_z(0)
     take_y(1)
     take_x(1)
-    take_z(0)
     serve(1, 0)
+    launch(3)
+    take_z(1)
     take_y(2)
-    take_z(1)
     take_x(2)
     serve(0, 0)
+    take_z(2)
     take_y(3)
-    take_z(2)
     take_x(3)
     serve(2, 0)
     give(2, 0)
@@ -469,8 +478,9 @@
             for copy in back(a, u):
                 copy.wait_send()
     for c in range(CHUNKS):
-        hop_x(c).wait_send()
-        hop_y(c).wait_send()
+        if c == CHUNKS - 1:
+            hop_x(c).wait_send()
+            hop_y(c).wait_send()
         hop_z(c).wait_send()
         hop_far(c, 1, px).wait_send()
     for copy in slot_copies:

time: 108 us -> 107 us (level)
  no operation moved by 1% of the time
where the time goes in v7:
time: 107 us
  Pallas kernels  101 us (94%)
  local copies, waits for them, and re-layouts  2.75 us (3%)
  other arithmetic  2.42 us (2%)
    pallas_call x1, Pallas kernels, fused_body(): pl.pallas_call(functools.partial(fused_kernel, n, reps), out_shape=jax.Sh...  101 us

profile of v7, /device:TPU:5, one launch (start us, length us, event | category | flops | bytes accessed | tf_op | source)
XLA Modules:
  0.0 106.6 jit_solution(4211501722065754208)
XLA Ops:
  0.0 0.1 stack.23
  0.1 0.7 compare_bitcast_fusion
  0.7 0.7 and_select_fusion
  1.4 0.7 fusion.2
  2.1 0.1 fusion.3
  2.1 0.2 reduce_window_sum.11
  2.3 0.2 select_reduce_fusion
  2.5 0.6 pad.4.slots
  3.1 101.4 %shard_map.46 = bf16[512,768]{1,0:T(8,128)(2,1)} custom-call(bf16[512,1024]{1,0:T(8,128)(2,1)} %left_hbm.1, bf16[8,256,1792]{2,1,0:T(8,128)(2,1)} %bitcast.13, s32[8,128]{1,0:T(8,128)} %pad.4.slots, s32[1,512]{1,0:T(1,128)} %bitcast.14), custom_call_target="tpu_custom_call" | custom-call | flops 11744051200 | bytes 9175040 | tf_op jit(solution)/shard_map/pallas_call | solution.py:537
  104.5 2.1 %copy.6 = bf16[512,768]{1,0:T(8,128)(2,1)} copy(bf16[512,768]{1,0:T(8,128)(2,1)} %shard_map.46) | data formatting | bytes 1572864
  (1 shorter events, 0.0 us)
